TPU v7x, 256 devices: a whole 4x4x8 slice. The times are simulated.
256 devices in a mesh: segment: 8 (over y, core), neuron: 32 (over z, x).
Axes of the slice: x: 4, y: 4, z: 8, core: 2. Of those that a mesh axis runs over, the one named last changes fastest.
Arguments:
- samples: bfloat16 [384, 65536], P(None, 'neuron'), may hold values from -6 to 6
- batch_of: int32 [384], replicated, may hold values from 0 to 2, as said below
- weights: bfloat16 [16, 512, 5, 128, 128], P('segment', 'neuron'), may hold values from -0.375 to 0.375
- block_offset: int32 [16, 512, 5], P('segment', 'neuron'), may hold values from -4 to 4, as said below
- block_count: int32 [16, 512], P('segment', 'neuron'), may hold values from 3 to 5
- bias: float32 [16, 65536], P('segment', 'neuron'), may hold values from -0.4 to 0.2
Outputs:
- section_out: bfloat16 [8, 3, 128, 65536], P('segment', None, None, 'neuron')
Inputs may be any that keep to these rules, and one draw needn't show every extreme that they name: `block_offset`: the 5 offsets of one block row are distinct. `batch_of`: each of the 3 micro-batches holds exactly 128 samples.
All inputs are finite; a program needn't handle non-finite values.
Results may differ from a plain program's by a relative error of at most 0.029.
Values may be sent and summed in bfloat16 or wider, within the bound.
A program may use at most 64 MiB of HBM per device.

v0:
```python
import jax
import jax.numpy as jnp
from jax import lax
from jax.sharding import PartitionSpec as P

BLOCK = 128
KMAX = 5
REACH = 4
LPS = 2
S = 128
NMB = 3


def with_halo(block, sides, width):
    for axis, dim in sides:
        count = lax.axis_size(axis)
        forward = [(i, i + 1) for i in range(count - 1)]
        backward = [(target, source) for source, target in forward]
        low = lax.ppermute(
            lax.slice_in_dim(block, block.shape[dim] - width, None, axis=dim), axis, forward
        )
        high = lax.ppermute(lax.slice_in_dim(block, 0, width, axis=dim), axis, backward)
        block = jnp.concatenate([low, block, high], axis=dim)
    return block


def passed_along(value, axis, steps):
    count = lax.axis_size(axis)
    initial, last = (max(0, -steps), min(count, count - steps))
    return lax.ppermute(value, axis, [(source, source + steps) for source in range(initial, last)])


def neuron_layer(current, weight, offset, count, bias_row):
    block_total = weight.shape[0]
    block_width = weight.shape[2]
    padded = with_halo(current, (("neuron", 0),), REACH)
    live_slots = jnp.arange(KMAX, dtype=jnp.int32)[None, :] < count[:, None]
    summed = jnp.zeros(current.shape, jnp.float32)
    for shift_no in range(2 * REACH + 1):
        chosen = (offset == shift_no - REACH) & live_slots
        dense = jnp.sum(
            jnp.where(chosen[:, :, None, None], weight, jnp.zeros((), weight.dtype)),
            axis=1,
            dtype=weight.dtype,
        )
        moved = padded[shift_no : shift_no + block_total]
        summed = summed + jnp.einsum(
            "jrc,jce->jre", moved, dense, preferred_element_type=jnp.float32
        )
    bias_blocks = bias_row.reshape(block_total, 1, block_width)
    return jnp.maximum(summed + bias_blocks, 0.0).astype(jnp.bfloat16)


def on_device(samples, batch_of, weights, block_offset, block_count, bias):
    segment_count = lax.axis_size("segment")
    segment_idx = lax.axis_index("segment")
    splits = 1
    batch_rows = S // splits
    pieces = NMB * splits
    local_width = samples.shape[1]
    local_blocks = local_width // BLOCK
    order = jnp.argsort(batch_of, stable=True).reshape(pieces, batch_rows)
    sample_blocks = samples.reshape(samples.shape[0], local_blocks, BLOCK).transpose(1, 0, 2)

    def section(current):
        for layer_no in range(LPS):
            current = neuron_layer(
                current,
                weights[layer_no],
                block_offset[layer_no],
                block_count[layer_no],
                bias[layer_no],
            )
        return current

    def advance(tick_no, carry):
        incoming, stored = carry
        entry_no = jnp.clip(tick_no, 0, pieces - 1)
        fresh = jnp.take(
            sample_blocks, lax.dynamic_index_in_dim(order, entry_no, 0, keepdims=False), axis=1
        )
        current = jnp.where(segment_idx == 0, fresh, incoming)
        result = section(current)
        piece_no = tick_no - segment_idx
        valid = (piece_no >= 0) & (piece_no < pieces)
        slot_no = jnp.clip(piece_no, 0, pieces - 1)
        previous = lax.dynamic_index_in_dim(stored, slot_no, 0, keepdims=False)
        stored = lax.dynamic_update_index_in_dim(
            stored, jnp.where(valid, result, previous), slot_no, 0
        )
        incoming = passed_along(result, "segment", 1)
        return (incoming, stored)

    start = (
        jnp.zeros((local_blocks, batch_rows, BLOCK), jnp.bfloat16),
        jnp.zeros((pieces, local_blocks, batch_rows, BLOCK), jnp.bfloat16),
    )
    _, stored = lax.fori_loop(0, pieces + segment_count - 1, advance, start)
    stored = stored.reshape(NMB, splits, local_blocks, batch_rows, BLOCK).transpose(0, 1, 3, 2, 4)
    return stored.reshape(1, NMB, S, local_width)


def solution(mesh):
    return jax.shard_map(
        on_device,
        mesh=mesh,
        in_specs=(
            P(None, "neuron"),
            P(),
            P("segment", "neuron", None, None, None),
            P("segment", "neuron", None),
            P("segment", "neuron"),
            P("segment", "neuron"),
        ),
        out_specs=P("segment", None, None, "neuron"),
        check_vma=False,
    )
```

profile of v0, /device:TPU:118, one launch (start us, length us, event | category | flops | bytes accessed | tf_op | source)
XLA Modules:
  0.0 553.1 jit_solution(14240029609240305401)
XLA Ops:
  2.4 8.9 %fusion.38 = (bf16[16,128,128]{2,1,0:T(8,128)(2,1)}, bf16[16,128,128]{2,1,0:T(8,128)(2,1)}, bf16[16,128,128]{2,1,0:T(8,128)(2,1)}, bf16[16,128,128]{2,1,0:T(8,12...) fusion(pred[16,5]{1,0:T(8,128)(4,1)S(1)} %copy.48, ...), kind=kLoop, calls=%fused_computation.66 | loop fusion | flops 21233664 | bytes 9962192 | tf_op jit(solution)/shard_map/while/body/eval_jaxpr/reduce_sum | solution.py:41
  12.3 9.0 %fusion.39 = (bf16[16,128,128]{2,1,0:T(8,128)(2,1)}, bf16[16,128,128]{2,1,0:T(8,128)(2,1)}, bf16[16,128,128]{2,1,0:T(8,128)(2,1)}, bf16[16,128,128]{2,1,0:T(8,12...) fusion(pred[16,5]{1,0:T(8,128)(4,1)S(1)} %copy.49, ...), kind=kLoop, calls=%fused_computation.67 | loop fusion | flops 21233664 | bytes 9962192 | tf_op jit(solution)/shard_map/while/body/eval_jaxpr/reduce_sum | solution.py:41
  24.1 3.8 sort.17
  28.4 521.7 %while.18 = (s32[]{:T(128)}, bf16[16,128,128]{2,1,0:T(8,128)(2,1)S(1)}, bf16[3,16,128,128]{3,2,1,0:T(8,128)(2,1)S(1)}, pred[]{:T(512)}, s32[3,128]{1,0:T(4,128)S...) while((s32[]{:T(128)}, ...), condition=%wide.region_20.21_spmd, body=%wide.region_19.20_spmd.sunk | while | flops 1235486848 | bytes 101244688 | solution.py:98
  30.8 5.0 collective-permute-start.1
  42.4 3.7 collective-permute-done
  52.5 4.3 collective-permute-start.3
  61.9 5.4 collective-permute-done.2
  74.2 8.6 %collective-permute-done.4 = bf16[16,128,128]{2,1,0:T(8,128)(2,1)S(1)} collective-permute-done((bf16[16,128,128]{2,1,0:T(8,128)(2,1)S(1)}, bf16[16,128,128]{2,1,0:T(8,128)(2,1)S(1)}, u32[]{:S(2)}, u32[]{:S(2)}) %collective-permute-start.4) | collective-permute-done | bytes 524320 | tf_op jit(solution)/shard_map/while/body/eval_jaxpr/ppermute | solution.py:30
  85.1 2.8 collective-permute-start.1
  87.9 3.1 collective-permute-start
  96.0 2.2 collective-permute-done
  104.7 4.0 collective-permute-start.3
  114.1 5.2 collective-permute-done.2
  126.1 8.6 %collective-permute-done.4 = bf16[16,128,128]{2,1,0:T(8,128)(2,1)S(1)} collective-permute-done((bf16[16,128,128]{2,1,0:T(8,128)(2,1)S(1)}, bf16[16,128,128]{2,1,0:T(8,128)(2,1)S(1)}, u32[]{:S(2)}, u32[]{:S(2)}) %collective-permute-start.4) | collective-permute-done | bytes 524320 | tf_op jit(solution)/shard_map/while/body/eval_jaxpr/ppermute | solution.py:30
  134.7 2.1 gather_fusion
  137.0 2.8 collective-permute-start.1
  139.8 3.1 collective-permute-start
  147.9 2.2 collective-permute-done
  156.6 4.0 collective-permute-start.3
  166.0 5.2 collective-permute-done.2
  178.0 8.6 %collective-permute-done.4 = bf16[16,128,128]{2,1,0:T(8,128)(2,1)S(1)} collective-permute-done((bf16[16,128,128]{2,1,0:T(8,128)(2,1)S(1)}, bf16[16,128,128]{2,1,0:T(8,128)(2,1)S(1)}, u32[]{:S(2)}, u32[]{:S(2)}) %collective-permute-start.4) | collective-permute-done | bytes 524320 | tf_op jit(solution)/shard_map/while/body/eval_jaxpr/ppermute | solution.py:30
  189.0 2.8 collective-permute-start.1
  191.8 3.1 collective-permute-start
  199.8 2.2 collective-permute-done
  208.6 4.0 collective-permute-start.3
  217.9 5.2 collective-permute-done.2
  230.0 8.6 %collective-permute-done.4 = bf16[16,128,128]{2,1,0:T(8,128)(2,1)S(1)} collective-permute-done((bf16[16,128,128]{2,1,0:T(8,128)(2,1)S(1)}, bf16[16,128,128]{2,1,0:T(8,128)(2,1)S(1)}, u32[]{:S(2)}, u32[]{:S(2)}) %collective-permute-start.4) | collective-permute-done | bytes 524320 | tf_op jit(solution)/shard_map/while/body/eval_jaxpr/ppermute | solution.py:30
  240.9 2.8 collective-permute-start.1
  243.7 3.1 collective-permute-start
  251.8 2.2 collective-permute-done
  260.5 4.0 collective-permute-start.3
  269.9 5.2 collective-permute-done.2
  281.9 8.6 %collective-permute-done.4 = bf16[16,128,128]{2,1,0:T(8,128)(2,1)S(1)} collective-permute-done((bf16[16,128,128]{2,1,0:T(8,128)(2,1)S(1)}, bf16[16,128,128]{2,1,0:T(8,128)(2,1)S(1)}, u32[]{:S(2)}, u32[]{:S(2)}) %collective-permute-start.4) | collective-permute-done | bytes 524320 | tf_op jit(solution)/shard_map/while/body/eval_jaxpr/ppermute | solution.py:30
  292.8 2.8 collective-permute-start.1
  295.6 3.1 collective-permute-start
  303.7 2.2 collective-permute-done
  312.4 4.0 collective-permute-start.3
  321.8 5.2 collective-permute-done.2
  333.8 8.6 %collective-permute-done.4 = bf16[16,128,128]{2,1,0:T(8,128)(2,1)S(1)} collective-permute-done((bf16[16,128,128]{2,1,0:T(8,128)(2,1)S(1)}, bf16[16,128,128]{2,1,0:T(8,128)(2,1)S(1)}, u32[]{:S(2)}, u32[]{:S(2)}) %collective-permute-start.4) | collective-permute-done | bytes 524320 | tf_op jit(solution)/shard_map/while/body/eval_jaxpr/ppermute | solution.py:30
  344.7 2.8 collective-permute-start.1
  347.5 3.1 collective-permute-start
  355.6 2.2 collective-permute-done
  364.3 4.0 collective-permute-start.3
  373.7 5.2 collective-permute-done.2
  385.7 8.6 %collective-permute-done.4 = bf16[16,128,128]{2,1,0:T(8,128)(2,1)S(1)} collective-permute-done((bf16[16,128,128]{2,1,0:T(8,128)(2,1)S(1)}, bf16[16,128,128]{2,1,0:T(8,128)(2,1)S(1)}, u32[]{:S(2)}, u32[]{:S(2)}) %collective-permute-start.4) | collective-permute-done | bytes 524320 | tf_op jit(solution)/shard_map/while/body/eval_jaxpr/ppermute | solution.py:30
  396.7 2.8 collective-permute-start.1
  399.5 3.1 collective-permute-start
  407.5 2.2 collective-permute-done
  416.2 4.0 collective-permute-start.3
  425.6 5.2 collective-permute-done.2
  437.6 8.6 %collective-permute-done.4 = bf16[16,128,128]{2,1,0:T(8,128)(2,1)S(1)} collective-permute-done((bf16[16,128,128]{2,1,0:T(8,128)(2,1)S(1)}, bf16[16,128,128]{2,1,0:T(8,128)(2,1)S(1)}, u32[]{:S(2)}, u32[]{:S(2)}) %collective-permute-start.4) | collective-permute-done | bytes 524320 | tf_op jit(solution)/shard_map/while/body/eval_jaxpr/ppermute | solution.py:30
  448.6 2.8 collective-permute-start.1
  451.4 3.1 collective-permute-start
  459.5 2.2 collective-permute-done
  468.2 4.0 collective-permute-start.3
  477.6 5.2 collective-permute-done.2
  489.6 8.6 %collective-permute-done.4 = bf16[16,128,128]{2,1,0:T(8,128)(2,1)S(1)} collective-permute-done((bf16[16,128,128]{2,1,0:T(8,128)(2,1)S(1)}, bf16[16,128,128]{2,1,0:T(8,128)(2,1)S(1)}, u32[]{:S(2)}, u32[]{:S(2)}) %collective-permute-start.4) | collective-permute-done | bytes 524320 | tf_op jit(solution)/shard_map/while/body/eval_jaxpr/ppermute | solution.py:30
  500.5 2.8 collective-permute-start.1
  503.3 3.1 collective-permute-start
  511.4 2.2 collective-permute-done
  520.1 4.0 collective-permute-start.3
  529.5 5.2 collective-permute-done.2
  541.5 8.6 %collective-permute-done.4 = bf16[16,128,128]{2,1,0:T(8,128)(2,1)S(1)} collective-permute-done((bf16[16,128,128]{2,1,0:T(8,128)(2,1)S(1)}, bf16[16,128,128]{2,1,0:T(8,128)(2,1)S(1)}, u32[]{:S(2)}, u32[]{:S(2)}) %collective-permute-start.4) | collective-permute-done | bytes 524320 | tf_op jit(solution)/shard_map/while/body/eval_jaxpr/ppermute | solution.py:30
  (684 shorter events, 265.8 us)
Async XLA Ops:
  12.3 9.0 %copy-start.2 = (bf16[384,2048]{1,0:T(8,128)(2,1)S(1)}, bf16[384,2048]{1,0:T(8,128)(2,1)}, u32[]{:S(2)}) copy-start(bf16[384,2048]{1,0:T(8,128)(2,1)} %param.8) | copy-start | bytes 4718596
  30.5 7.1 %copy-start.1 = (bf16[16,128,128]{2,1,0:T(8,128)(2,1)S(1)}, bf16[16,128,128]{2,1,0:T(8,128)(2,1)}, u32[]{:S(2)}) copy-start(bf16[16,128,128]{2,1,0:T(8,128)(2,1)} %get-tuple-element.748) | copy-start | bytes 1572868 | tf_op jit(solution)/shard_map/while
  30.8 7.7 %collective-permute-start.1 = (bf16[4,128,128]{2,1,0:T(8,128)(2,1)S(1)}, bf16[4,128,128]{2,1,0:T(8,128)(2,1)}, u32[]{:S(2)}, u32[]{:S(2)}) collective-permute-start(bf16[4,128,128]{2,1,0:T(8,128)(2,1)S(1)} %get-tuple-element.672), channel_id=1, source_target_pairs={{0,1},{1,2},{2,3},{3,4},{4,5},{5,6},{6,7},{7,8},{8,9},{9,10},{10,1... | collective-permute-start | bytes 393224 | tf_op jit(solution)/shard_map/while/body/eval_jaxpr/ppermute | solution.py:19
  35.7 10.3 %collective-permute-start = (bf16[4,128,128]{2,1,0:T(8,128)(2,1)S(1)}, bf16[4,128,128]{2,1,0:T(8,128)(2,1)}, u32[]{:S(2)}, u32[]{:S(2)}) collective-permute-start(bf16[4,128,128]{2,1,0:T(8,128)(2,1)S(1)} %get-tuple-element.671), channel_id=1, source_target_pairs={{1,0},{2,1},{3,2},{4,3},{5,4},{6,5},{7,6},{8,7},{9,8},{10,9},{11,1... | collective-permute-start | bytes 393224 | tf_op jit(solution)/shard_map/while/body/eval_jaxpr/ppermute | solution.py:22
  52.5 7.0 %copy-start.8 = (bf16[16,128,128]{2,1,0:T(8,128)(2,1)S(1)}, bf16[16,128,128]{2,1,0:T(8,128)(2,1)}, u32[]{:S(2)}) copy-start(bf16[16,128,128]{2,1,0:T(8,128)(2,1)} %get-tuple-element.755) | copy-start | bytes 1572868 | tf_op jit(solution)/shard_map/while
  52.5 7.0 %collective-permute-start.3 = (bf16[4,128,128]{2,1,0:T(8,128)(2,1)S(1)}, bf16[4,128,128]{2,1,0:T(8,128)(2,1)S(1)}, u32[]{:S(2)}, u32[]{:S(2)}) collective-permute-start(bf16[4,128,128]{2,1,0:T(8,128)(2,1)S(1)} %get-tuple-element.675), channel_id=1, source_target_pairs={{0,1},{1,2},{2,3},{3,4},{4,5},{5,6},{6,7},{7,8},{8,9},{9,10},{10,1... | collective-permute-start | bytes 393224 | tf_op jit(solution)/shard_map/while/body/eval_jaxpr/ppermute | solution.py:19
  57.2 10.2 %collective-permute-start.2 = (bf16[4,128,128]{2,1,0:T(8,128)(2,1)S(1)}, bf16[4,128,128]{2,1,0:T(8,128)(2,1)S(1)}, u32[]{:S(2)}, u32[]{:S(2)}) collective-permute-start(bf16[4,128,128]{2,1,0:T(8,128)(2,1)S(1)} %get-tuple-element.674), channel_id=1, source_target_pairs={{1,0},{2,1},{3,2},{4,3},{5,4},{6,5},{7,6},{8,7},{9,8},{10,9},{11,1... | collective-permute-start | bytes 393224 | tf_op jit(solution)/shard_map/while/body/eval_jaxpr/ppermute | solution.py:22
  72.2 10.5 %collective-permute-start.4 = (bf16[16,128,128]{2,1,0:T(8,128)(2,1)S(1)}, bf16[16,128,128]{2,1,0:T(8,128)(2,1)S(1)}, u32[]{:S(2)}, u32[]{:S(2)}) collective-permute-start(bf16[16,128,128]{2,1,0:T(8,128)(2,1)S(1)} %get-tuple-element.676), channel_id=1, source_target_pairs={{0,32},{32,64},{64,96},{96,128},{128,160},{160,192},{192,224},{1,3... | collective-permute-start | bytes 1572872 | tf_op jit(solution)/shard_map/while/body/eval_jaxpr/ppermute | solution.py:30
  84.9 6.1 %copy-start.1 = (bf16[16,128,128]{2,1,0:T(8,128)(2,1)S(1)}, bf16[16,128,128]{2,1,0:T(8,128)(2,1)}, u32[]{:S(2)}) copy-start(bf16[16,128,128]{2,1,0:T(8,128)(2,1)} %get-tuple-element.748) | copy-start | bytes 1572868 | tf_op jit(solution)/shard_map/while
  85.1 7.0 %collective-permute-start.1 = (bf16[4,128,128]{2,1,0:T(8,128)(2,1)S(1)}, bf16[4,128,128]{2,1,0:T(8,128)(2,1)}, u32[]{:S(2)}, u32[]{:S(2)}) collective-permute-start(bf16[4,128,128]{2,1,0:T(8,128)(2,1)S(1)} %get-tuple-element.672), channel_id=1, source_target_pairs={{0,1},{1,2},{2,3},{3,4},{4,5},{5,6},{6,7},{7,8},{8,9},{9,10},{10,1... | collective-permute-start | bytes 393224 | tf_op jit(solution)/shard_map/while/body/eval_jaxpr/ppermute | solution.py:19
  87.9 10.3 %collective-permute-start = (bf16[4,128,128]{2,1,0:T(8,128)(2,1)S(1)}, bf16[4,128,128]{2,1,0:T(8,128)(2,1)}, u32[]{:S(2)}, u32[]{:S(2)}) collective-permute-start(bf16[4,128,128]{2,1,0:T(8,128)(2,1)S(1)} %get-tuple-element.671), channel_id=1, source_target_pairs={{1,0},{2,1},{3,2},{4,3},{5,4},{6,5},{7,6},{8,7},{9,8},{10,9},{11,1... | collective-permute-start | bytes 393224 | tf_op jit(solution)/shard_map/while/body/eval_jaxpr/ppermute | solution.py:22
  104.7 7.0 %copy-start.8 = (bf16[16,128,128]{2,1,0:T(8,128)(2,1)S(1)}, bf16[16,128,128]{2,1,0:T(8,128)(2,1)}, u32[]{:S(2)}) copy-start(bf16[16,128,128]{2,1,0:T(8,128)(2,1)} %get-tuple-element.755) | copy-start | bytes 1572868 | tf_op jit(solution)/shard_map/while
  104.7 7.0 %collective-permute-start.3 = (bf16[4,128,128]{2,1,0:T(8,128)(2,1)S(1)}, bf16[4,128,128]{2,1,0:T(8,128)(2,1)S(1)}, u32[]{:S(2)}, u32[]{:S(2)}) collective-permute-start(bf16[4,128,128]{2,1,0:T(8,128)(2,1)S(1)} %get-tuple-element.675), channel_id=1, source_target_pairs={{0,1},{1,2},{2,3},{3,4},{4,5},{5,6},{6,7},{7,8},{8,9},{9,10},{10,1... | collective-permute-start | bytes 393224 | tf_op jit(solution)/shard_map/while/body/eval_jaxpr/ppermute | solution.py:19
  109.1 10.2 %collective-permute-start.2 = (bf16[4,128,128]{2,1,0:T(8,128)(2,1)S(1)}, bf16[4,128,128]{2,1,0:T(8,128)(2,1)S(1)}, u32[]{:S(2)}, u32[]{:S(2)}) collective-permute-start(bf16[4,128,128]{2,1,0:T(8,128)(2,1)S(1)} %get-tuple-element.674), channel_id=1, source_target_pairs={{1,0},{2,1},{3,2},{4,3},{5,4},{6,5},{7,6},{8,7},{9,8},{10,9},{11,1... | collective-permute-start | bytes 393224 | tf_op jit(solution)/shard_map/while/body/eval_jaxpr/ppermute | solution.py:22
  124.2 10.5 %collective-permute-start.4 = (bf16[16,128,128]{2,1,0:T(8,128)(2,1)S(1)}, bf16[16,128,128]{2,1,0:T(8,128)(2,1)S(1)}, u32[]{:S(2)}, u32[]{:S(2)}) collective-permute-start(bf16[16,128,128]{2,1,0:T(8,128)(2,1)S(1)} %get-tuple-element.676), channel_id=1, source_target_pairs={{0,32},{32,64},{64,96},{96,128},{128,160},{160,192},{192,224},{1,3... | collective-permute-start | bytes 1572872 | tf_op jit(solution)/shard_map/while/body/eval_jaxpr/ppermute | solution.py:30
  136.8 6.1 %copy-start.1 = (bf16[16,128,128]{2,1,0:T(8,128)(2,1)S(1)}, bf16[16,128,128]{2,1,0:T(8,128)(2,1)}, u32[]{:S(2)}) copy-start(bf16[16,128,128]{2,1,0:T(8,128)(2,1)} %get-tuple-element.748) | copy-start | bytes 1572868 | tf_op jit(solution)/shard_map/while
  137.0 7.0 %collective-permute-start.1 = (bf16[4,128,128]{2,1,0:T(8,128)(2,1)S(1)}, bf16[4,128,128]{2,1,0:T(8,128)(2,1)}, u32[]{:S(2)}, u32[]{:S(2)}) collective-permute-start(bf16[4,128,128]{2,1,0:T(8,128)(2,1)S(1)} %get-tuple-element.672), channel_id=1, source_target_pairs={{0,1},{1,2},{2,3},{3,4},{4,5},{5,6},{6,7},{7,8},{8,9},{9,10},{10,1... | collective-permute-start | bytes 393224 | tf_op jit(solution)/shard_map/while/body/eval_jaxpr/ppermute | solution.py:19
  139.8 10.3 %collective-permute-start = (bf16[4,128,128]{2,1,0:T(8,128)(2,1)S(1)}, bf16[4,128,128]{2,1,0:T(8,128)(2,1)}, u32[]{:S(2)}, u32[]{:S(2)}) collective-permute-start(bf16[4,128,128]{2,1,0:T(8,128)(2,1)S(1)} %get-tuple-element.671), channel_id=1, source_target_pairs={{1,0},{2,1},{3,2},{4,3},{5,4},{6,5},{7,6},{8,7},{9,8},{10,9},{11,1... | collective-permute-start | bytes 393224 | tf_op jit(solution)/shard_map/while/body/eval_jaxpr/ppermute | solution.py:22
  156.6 7.0 %copy-start.8 = (bf16[16,128,128]{2,1,0:T(8,128)(2,1)S(1)}, bf16[16,128,128]{2,1,0:T(8,128)(2,1)}, u32[]{:S(2)}) copy-start(bf16[16,128,128]{2,1,0:T(8,128)(2,1)} %get-tuple-element.755) | copy-start | bytes 1572868 | tf_op jit(solution)/shard_map/while
  156.6 7.0 %collective-permute-start.3 = (bf16[4,128,128]{2,1,0:T(8,128)(2,1)S(1)}, bf16[4,128,128]{2,1,0:T(8,128)(2,1)S(1)}, u32[]{:S(2)}, u32[]{:S(2)}) collective-permute-start(bf16[4,128,128]{2,1,0:T(8,128)(2,1)S(1)} %get-tuple-element.675), channel_id=1, source_target_pairs={{0,1},{1,2},{2,3},{3,4},{4,5},{5,6},{6,7},{7,8},{8,9},{9,10},{10,1... | collective-permute-start | bytes 393224 | tf_op jit(solution)/shard_map/while/body/eval_jaxpr/ppermute | solution.py:19
  161.0 10.2 %collective-permute-start.2 = (bf16[4,128,128]{2,1,0:T(8,128)(2,1)S(1)}, bf16[4,128,128]{2,1,0:T(8,128)(2,1)S(1)}, u32[]{:S(2)}, u32[]{:S(2)}) collective-permute-start(bf16[4,128,128]{2,1,0:T(8,128)(2,1)S(1)} %get-tuple-element.674), channel_id=1, source_target_pairs={{1,0},{2,1},{3,2},{4,3},{5,4},{6,5},{7,6},{8,7},{9,8},{10,9},{11,1... | collective-permute-start | bytes 393224 | tf_op jit(solution)/shard_map/while/body/eval_jaxpr/ppermute | solution.py:22
  176.1 10.5 %collective-permute-start.4 = (bf16[16,128,128]{2,1,0:T(8,128)(2,1)S(1)}, bf16[16,128,128]{2,1,0:T(8,128)(2,1)S(1)}, u32[]{:S(2)}, u32[]{:S(2)}) collective-permute-start(bf16[16,128,128]{2,1,0:T(8,128)(2,1)S(1)} %get-tuple-element.676), channel_id=1, source_target_pairs={{0,32},{32,64},{64,96},{96,128},{128,160},{160,192},{192,224},{1,3... | collective-permute-start | bytes 1572872 | tf_op jit(solution)/shard_map/while/body/eval_jaxpr/ppermute | solution.py:30
  189.0 7.0 %collective-permute-start.1 = (bf16[4,128,128]{2,1,0:T(8,128)(2,1)S(1)}, bf16[4,128,128]{2,1,0:T(8,128)(2,1)}, u32[]{:S(2)}, u32[]{:S(2)}) collective-permute-start(bf16[4,128,128]{2,1,0:T(8,128)(2,1)S(1)} %get-tuple-element.672), channel_id=1, source_target_pairs={{0,1},{1,2},{2,3},{3,4},{4,5},{5,6},{6,7},{7,8},{8,9},{9,10},{10,1... | collective-permute-start | bytes 393224 | tf_op jit(solution)/shard_map/while/body/eval_jaxpr/ppermute | solution.py:19
  191.8 10.3 %collective-permute-start = (bf16[4,128,128]{2,1,0:T(8,128)(2,1)S(1)}, bf16[4,128,128]{2,1,0:T(8,128)(2,1)}, u32[]{:S(2)}, u32[]{:S(2)}) collective-permute-start(bf16[4,128,128]{2,1,0:T(8,128)(2,1)S(1)} %get-tuple-element.671), channel_id=1, source_target_pairs={{1,0},{2,1},{3,2},{4,3},{5,4},{6,5},{7,6},{8,7},{9,8},{10,9},{11,1... | collective-permute-start | bytes 393224 | tf_op jit(solution)/shard_map/while/body/eval_jaxpr/ppermute | solution.py:22
  208.5 7.0 %copy-start.8 = (bf16[16,128,128]{2,1,0:T(8,128)(2,1)S(1)}, bf16[16,128,128]{2,1,0:T(8,128)(2,1)}, u32[]{:S(2)}) copy-start(bf16[16,128,128]{2,1,0:T(8,128)(2,1)} %get-tuple-element.755) | copy-start | bytes 1572868 | tf_op jit(solution)/shard_map/while
  208.6 7.0 %collective-permute-start.3 = (bf16[4,128,128]{2,1,0:T(8,128)(2,1)S(1)}, bf16[4,128,128]{2,1,0:T(8,128)(2,1)S(1)}, u32[]{:S(2)}, u32[]{:S(2)}) collective-permute-start(bf16[4,128,128]{2,1,0:T(8,128)(2,1)S(1)} %get-tuple-element.675), channel_id=1, source_target_pairs={{0,1},{1,2},{2,3},{3,4},{4,5},{5,6},{6,7},{7,8},{8,9},{9,10},{10,1... | collective-permute-start | bytes 393224 | tf_op jit(solution)/shard_map/while/body/eval_jaxpr/ppermute | solution.py:19
  212.9 10.2 %collective-permute-start.2 = (bf16[4,128,128]{2,1,0:T(8,128)(2,1)S(1)}, bf16[4,128,128]{2,1,0:T(8,128)(2,1)S(1)}, u32[]{:S(2)}, u32[]{:S(2)}) collective-permute-start(bf16[4,128,128]{2,1,0:T(8,128)(2,1)S(1)} %get-tuple-element.674), channel_id=1, source_target_pairs={{1,0},{2,1},{3,2},{4,3},{5,4},{6,5},{7,6},{8,7},{9,8},{10,9},{11,1... | collective-permute-start | bytes 393224 | tf_op jit(solution)/shard_map/while/body/eval_jaxpr/ppermute | solution.py:22
  228.0 10.5 %collective-permute-start.4 = (bf16[16,128,128]{2,1,0:T(8,128)(2,1)S(1)}, bf16[16,128,128]{2,1,0:T(8,128)(2,1)S(1)}, u32[]{:S(2)}, u32[]{:S(2)}) collective-permute-start(bf16[16,128,128]{2,1,0:T(8,128)(2,1)S(1)} %get-tuple-element.676), channel_id=1, source_target_pairs={{0,32},{32,64},{64,96},{96,128},{128,160},{160,192},{192,224},{1,3... | collective-permute-start | bytes 1572872 | tf_op jit(solution)/shard_map/while/body/eval_jaxpr/ppermute | solution.py:30
  240.9 7.0 %collective-permute-start.1 = (bf16[4,128,128]{2,1,0:T(8,128)(2,1)S(1)}, bf16[4,128,128]{2,1,0:T(8,128)(2,1)}, u32[]{:S(2)}, u32[]{:S(2)}) collective-permute-start(bf16[4,128,128]{2,1,0:T(8,128)(2,1)S(1)} %get-tuple-element.672), channel_id=1, source_target_pairs={{0,1},{1,2},{2,3},{3,4},{4,5},{5,6},{6,7},{7,8},{8,9},{9,10},{10,1... | collective-permute-start | bytes 393224 | tf_op jit(solution)/shard_map/while/body/eval_jaxpr/ppermute | solution.py:19
  243.7 10.3 %collective-permute-start = (bf16[4,128,128]{2,1,0:T(8,128)(2,1)S(1)}, bf16[4,128,128]{2,1,0:T(8,128)(2,1)}, u32[]{:S(2)}, u32[]{:S(2)}) collective-permute-start(bf16[4,128,128]{2,1,0:T(8,128)(2,1)S(1)} %get-tuple-element.671), channel_id=1, source_target_pairs={{1,0},{2,1},{3,2},{4,3},{5,4},{6,5},{7,6},{8,7},{9,8},{10,9},{11,1... | collective-permute-start | bytes 393224 | tf_op jit(solution)/shard_map/while/body/eval_jaxpr/ppermute | solution.py:22
  260.4 7.0 %copy-start.8 = (bf16[16,128,128]{2,1,0:T(8,128)(2,1)S(1)}, bf16[16,128,128]{2,1,0:T(8,128)(2,1)}, u32[]{:S(2)}) copy-start(bf16[16,128,128]{2,1,0:T(8,128)(2,1)} %get-tuple-element.755) | copy-start | bytes 1572868 | tf_op jit(solution)/shard_map/while
  260.5 7.0 %collective-permute-start.3 = (bf16[4,128,128]{2,1,0:T(8,128)(2,1)S(1)}, bf16[4,128,128]{2,1,0:T(8,128)(2,1)S(1)}, u32[]{:S(2)}, u32[]{:S(2)}) collective-permute-start(bf16[4,128,128]{2,1,0:T(8,128)(2,1)S(1)} %get-tuple-element.675), channel_id=1, source_target_pairs={{0,1},{1,2},{2,3},{3,4},{4,5},{5,6},{6,7},{7,8},{8,9},{9,10},{10,1... | collective-permute-start | bytes 393224 | tf_op jit(solution)/shard_map/while/body/eval_jaxpr/ppermute | solution.py:19
  264.9 10.2 %collective-permute-start.2 = (bf16[4,128,128]{2,1,0:T(8,128)(2,1)S(1)}, bf16[4,128,128]{2,1,0:T(8,128)(2,1)S(1)}, u32[]{:S(2)}, u32[]{:S(2)}) collective-permute-start(bf16[4,128,128]{2,1,0:T(8,128)(2,1)S(1)} %get-tuple-element.674), channel_id=1, source_target_pairs={{1,0},{2,1},{3,2},{4,3},{5,4},{6,5},{7,6},{8,7},{9,8},{10,9},{11,1... | collective-permute-start | bytes 393224 | tf_op jit(solution)/shard_map/while/body/eval_jaxpr/ppermute | solution.py:22
  279.9 10.5 %collective-permute-start.4 = (bf16[16,128,128]{2,1,0:T(8,128)(2,1)S(1)}, bf16[16,128,128]{2,1,0:T(8,128)(2,1)S(1)}, u32[]{:S(2)}, u32[]{:S(2)}) collective-permute-start(bf16[16,128,128]{2,1,0:T(8,128)(2,1)S(1)} %get-tuple-element.676), channel_id=1, source_target_pairs={{0,32},{32,64},{64,96},{96,128},{128,160},{160,192},{192,224},{1,3... | collective-permute-start | bytes 1572872 | tf_op jit(solution)/shard_map/while/body/eval_jaxpr/ppermute | solution.py:30
  292.8 7.0 %collective-permute-start.1 = (bf16[4,128,128]{2,1,0:T(8,128)(2,1)S(1)}, bf16[4,128,128]{2,1,0:T(8,128)(2,1)}, u32[]{:S(2)}, u32[]{:S(2)}) collective-permute-start(bf16[4,128,128]{2,1,0:T(8,128)(2,1)S(1)} %get-tuple-element.672), channel_id=1, source_target_pairs={{0,1},{1,2},{2,3},{3,4},{4,5},{5,6},{6,7},{7,8},{8,9},{9,10},{10,1... | collective-permute-start | bytes 393224 | tf_op jit(solution)/shard_map/while/body/eval_jaxpr/ppermute | solution.py:19
  295.6 10.3 %collective-permute-start = (bf16[4,128,128]{2,1,0:T(8,128)(2,1)S(1)}, bf16[4,128,128]{2,1,0:T(8,128)(2,1)}, u32[]{:S(2)}, u32[]{:S(2)}) collective-permute-start(bf16[4,128,128]{2,1,0:T(8,128)(2,1)S(1)} %get-tuple-element.671), channel_id=1, source_target_pairs={{1,0},{2,1},{3,2},{4,3},{5,4},{6,5},{7,6},{8,7},{9,8},{10,9},{11,1... | collective-permute-start | bytes 393224 | tf_op jit(solution)/shard_map/while/body/eval_jaxpr/ppermute | solution.py:22
  312.4 7.0 %copy-start.8 = (bf16[16,128,128]{2,1,0:T(8,128)(2,1)S(1)}, bf16[16,128,128]{2,1,0:T(8,128)(2,1)}, u32[]{:S(2)}) copy-start(bf16[16,128,128]{2,1,0:T(8,128)(2,1)} %get-tuple-element.755) | copy-start | bytes 1572868 | tf_op jit(solution)/shard_map/while
  312.4 7.0 %collective-permute-start.3 = (bf16[4,128,128]{2,1,0:T(8,128)(2,1)S(1)}, bf16[4,128,128]{2,1,0:T(8,128)(2,1)S(1)}, u32[]{:S(2)}, u32[]{:S(2)}) collective-permute-start(bf16[4,128,128]{2,1,0:T(8,128)(2,1)S(1)} %get-tuple-element.675), channel_id=1, source_target_pairs={{0,1},{1,2},{2,3},{3,4},{4,5},{5,6},{6,7},{7,8},{8,9},{9,10},{10,1... | collective-permute-start | bytes 393224 | tf_op jit(solution)/shard_map/while/body/eval_jaxpr/ppermute | solution.py:19
  316.8 10.2 %collective-permute-start.2 = (bf16[4,128,128]{2,1,0:T(8,128)(2,1)S(1)}, bf16[4,128,128]{2,1,0:T(8,128)(2,1)S(1)}, u32[]{:S(2)}, u32[]{:S(2)}) collective-permute-start(bf16[4,128,128]{2,1,0:T(8,128)(2,1)S(1)} %get-tuple-element.674), channel_id=1, source_target_pairs={{1,0},{2,1},{3,2},{4,3},{5,4},{6,5},{7,6},{8,7},{9,8},{10,9},{11,1... | collective-permute-start | bytes 393224 | tf_op jit(solution)/shard_map/while/body/eval_jaxpr/ppermute | solution.py:22
  331.9 10.5 %collective-permute-start.4 = (bf16[16,128,128]{2,1,0:T(8,128)(2,1)S(1)}, bf16[16,128,128]{2,1,0:T(8,128)(2,1)S(1)}, u32[]{:S(2)}, u32[]{:S(2)}) collective-permute-start(bf16[16,128,128]{2,1,0:T(8,128)(2,1)S(1)} %get-tuple-element.676), channel_id=1, source_target_pairs={{0,32},{32,64},{64,96},{96,128},{128,160},{160,192},{192,224},{1,3... | collective-permute-start | bytes 1572872 | tf_op jit(solution)/shard_map/while/body/eval_jaxpr/ppermute | solution.py:30
  344.7 7.0 %collective-permute-start.1 = (bf16[4,128,128]{2,1,0:T(8,128)(2,1)S(1)}, bf16[4,128,128]{2,1,0:T(8,128)(2,1)}, u32[]{:S(2)}, u32[]{:S(2)}) collective-permute-start(bf16[4,128,128]{2,1,0:T(8,128)(2,1)S(1)} %get-tuple-element.672), channel_id=1, source_target_pairs={{0,1},{1,2},{2,3},{3,4},{4,5},{5,6},{6,7},{7,8},{8,9},{9,10},{10,1... | collective-permute-start | bytes 393224 | tf_op jit(solution)/shard_map/while/body/eval_jaxpr/ppermute | solution.py:19
  347.5 10.3 %collective-permute-start = (bf16[4,128,128]{2,1,0:T(8,128)(2,1)S(1)}, bf16[4,128,128]{2,1,0:T(8,128)(2,1)}, u32[]{:S(2)}, u32[]{:S(2)}) collective-permute-start(bf16[4,128,128]{2,1,0:T(8,128)(2,1)S(1)} %get-tuple-element.671), channel_id=1, source_target_pairs={{1,0},{2,1},{3,2},{4,3},{5,4},{6,5},{7,6},{8,7},{9,8},{10,9},{11,1... | collective-permute-start | bytes 393224 | tf_op jit(solution)/shard_map/while/body/eval_jaxpr/ppermute | solution.py:22
  364.3 7.0 %copy-start.8 = (bf16[16,128,128]{2,1,0:T(8,128)(2,1)S(1)}, bf16[16,128,128]{2,1,0:T(8,128)(2,1)}, u32[]{:S(2)}) copy-start(bf16[16,128,128]{2,1,0:T(8,128)(2,1)} %get-tuple-element.755) | copy-start | bytes 1572868 | tf_op jit(solution)/shard_map/while
  364.3 7.0 %collective-permute-start.3 = (bf16[4,128,128]{2,1,0:T(8,128)(2,1)S(1)}, bf16[4,128,128]{2,1,0:T(8,128)(2,1)S(1)}, u32[]{:S(2)}, u32[]{:S(2)}) collective-permute-start(bf16[4,128,128]{2,1,0:T(8,128)(2,1)S(1)} %get-tuple-element.675), channel_id=1, source_target_pairs={{0,1},{1,2},{2,3},{3,4},{4,5},{5,6},{6,7},{7,8},{8,9},{9,10},{10,1... | collective-permute-start | bytes 393224 | tf_op jit(solution)/shard_map/while/body/eval_jaxpr/ppermute | solution.py:19
  368.7 10.2 %collective-permute-start.2 = (bf16[4,128,128]{2,1,0:T(8,128)(2,1)S(1)}, bf16[4,128,128]{2,1,0:T(8,128)(2,1)S(1)}, u32[]{:S(2)}, u32[]{:S(2)}) collective-permute-start(bf16[4,128,128]{2,1,0:T(8,128)(2,1)S(1)} %get-tuple-element.674), channel_id=1, source_target_pairs={{1,0},{2,1},{3,2},{4,3},{5,4},{6,5},{7,6},{8,7},{9,8},{10,9},{11,1... | collective-permute-start | bytes 393224 | tf_op jit(solution)/shard_map/while/body/eval_jaxpr/ppermute | solution.py:22
  383.8 10.5 %collective-permute-start.4 = (bf16[16,128,128]{2,1,0:T(8,128)(2,1)S(1)}, bf16[16,128,128]{2,1,0:T(8,128)(2,1)S(1)}, u32[]{:S(2)}, u32[]{:S(2)}) collective-permute-start(bf16[16,128,128]{2,1,0:T(8,128)(2,1)S(1)} %get-tuple-element.676), channel_id=1, source_target_pairs={{0,32},{32,64},{64,96},{96,128},{128,160},{160,192},{192,224},{1,3... | collective-permute-start | bytes 1572872 | tf_op jit(solution)/shard_map/while/body/eval_jaxpr/ppermute | solution.py:30
  396.7 7.0 %collective-permute-start.1 = (bf16[4,128,128]{2,1,0:T(8,128)(2,1)S(1)}, bf16[4,128,128]{2,1,0:T(8,128)(2,1)}, u32[]{:S(2)}, u32[]{:S(2)}) collective-permute-start(bf16[4,128,128]{2,1,0:T(8,128)(2,1)S(1)} %get-tuple-element.672), channel_id=1, source_target_pairs={{0,1},{1,2},{2,3},{3,4},{4,5},{5,6},{6,7},{7,8},{8,9},{9,10},{10,1... | collective-permute-start | bytes 393224 | tf_op jit(solution)/shard_map/while/body/eval_jaxpr/ppermute | solution.py:19
  399.5 10.3 %collective-permute-start = (bf16[4,128,128]{2,1,0:T(8,128)(2,1)S(1)}, bf16[4,128,128]{2,1,0:T(8,128)(2,1)}, u32[]{:S(2)}, u32[]{:S(2)}) collective-permute-start(bf16[4,128,128]{2,1,0:T(8,128)(2,1)S(1)} %get-tuple-element.671), channel_id=1, source_target_pairs={{1,0},{2,1},{3,2},{4,3},{5,4},{6,5},{7,6},{8,7},{9,8},{10,9},{11,1... | collective-permute-start | bytes 393224 | tf_op jit(solution)/shard_map/while/body/eval_jaxpr/ppermute | solution.py:22
  416.2 7.0 %copy-start.8 = (bf16[16,128,128]{2,1,0:T(8,128)(2,1)S(1)}, bf16[16,128,128]{2,1,0:T(8,128)(2,1)}, u32[]{:S(2)}) copy-start(bf16[16,128,128]{2,1,0:T(8,128)(2,1)} %get-tuple-element.755) | copy-start | bytes 1572868 | tf_op jit(solution)/shard_map/while
  416.2 7.0 %collective-permute-start.3 = (bf16[4,128,128]{2,1,0:T(8,128)(2,1)S(1)}, bf16[4,128,128]{2,1,0:T(8,128)(2,1)S(1)}, u32[]{:S(2)}, u32[]{:S(2)}) collective-permute-start(bf16[4,128,128]{2,1,0:T(8,128)(2,1)S(1)} %get-tuple-element.675), channel_id=1, source_target_pairs={{0,1},{1,2},{2,3},{3,4},{4,5},{5,6},{6,7},{7,8},{8,9},{9,10},{10,1... | collective-permute-start | bytes 393224 | tf_op jit(solution)/shard_map/while/body/eval_jaxpr/ppermute | solution.py:19
  420.6 10.2 %collective-permute-start.2 = (bf16[4,128,128]{2,1,0:T(8,128)(2,1)S(1)}, bf16[4,128,128]{2,1,0:T(8,128)(2,1)S(1)}, u32[]{:S(2)}, u32[]{:S(2)}) collective-permute-start(bf16[4,128,128]{2,1,0:T(8,128)(2,1)S(1)} %get-tuple-element.674), channel_id=1, source_target_pairs={{1,0},{2,1},{3,2},{4,3},{5,4},{6,5},{7,6},{8,7},{9,8},{10,9},{11,1... | collective-permute-start | bytes 393224 | tf_op jit(solution)/shard_map/while/body/eval_jaxpr/ppermute | solution.py:22
  435.7 10.5 %collective-permute-start.4 = (bf16[16,128,128]{2,1,0:T(8,128)(2,1)S(1)}, bf16[16,128,128]{2,1,0:T(8,128)(2,1)S(1)}, u32[]{:S(2)}, u32[]{:S(2)}) collective-permute-start(bf16[16,128,128]{2,1,0:T(8,128)(2,1)S(1)} %get-tuple-element.676), channel_id=1, source_target_pairs={{0,32},{32,64},{64,96},{96,128},{128,160},{160,192},{192,224},{1,3... | collective-permute-start | bytes 1572872 | tf_op jit(solution)/shard_map/while/body/eval_jaxpr/ppermute | solution.py:30
  448.6 7.0 %collective-permute-start.1 = (bf16[4,128,128]{2,1,0:T(8,128)(2,1)S(1)}, bf16[4,128,128]{2,1,0:T(8,128)(2,1)}, u32[]{:S(2)}, u32[]{:S(2)}) collective-permute-start(bf16[4,128,128]{2,1,0:T(8,128)(2,1)S(1)} %get-tuple-element.672), channel_id=1, source_target_pairs={{0,1},{1,2},{2,3},{3,4},{4,5},{5,6},{6,7},{7,8},{8,9},{9,10},{10,1... | collective-permute-start | bytes 393224 | tf_op jit(solution)/shard_map/while/body/eval_jaxpr/ppermute | solution.py:19
  451.4 10.3 %collective-permute-start = (bf16[4,128,128]{2,1,0:T(8,128)(2,1)S(1)}, bf16[4,128,128]{2,1,0:T(8,128)(2,1)}, u32[]{:S(2)}, u32[]{:S(2)}) collective-permute-start(bf16[4,128,128]{2,1,0:T(8,128)(2,1)S(1)} %get-tuple-element.671), channel_id=1, source_target_pairs={{1,0},{2,1},{3,2},{4,3},{5,4},{6,5},{7,6},{8,7},{9,8},{10,9},{11,1... | collective-permute-start | bytes 393224 | tf_op jit(solution)/shard_map/while/body/eval_jaxpr/ppermute | solution.py:22
  468.1 7.0 %copy-start.8 = (bf16[16,128,128]{2,1,0:T(8,128)(2,1)S(1)}, bf16[16,128,128]{2,1,0:T(8,128)(2,1)}, u32[]{:S(2)}) copy-start(bf16[16,128,128]{2,1,0:T(8,128)(2,1)} %get-tuple-element.755) | copy-start | bytes 1572868 | tf_op jit(solution)/shard_map/while
  468.2 7.0 %collective-permute-start.3 = (bf16[4,128,128]{2,1,0:T(8,128)(2,1)S(1)}, bf16[4,128,128]{2,1,0:T(8,128)(2,1)S(1)}, u32[]{:S(2)}, u32[]{:S(2)}) collective-permute-start(bf16[4,128,128]{2,1,0:T(8,128)(2,1)S(1)} %get-tuple-element.675), channel_id=1, source_target_pairs={{0,1},{1,2},{2,3},{3,4},{4,5},{5,6},{6,7},{7,8},{8,9},{9,10},{10,1... | collective-permute-start | bytes 393224 | tf_op jit(solution)/shard_map/while/body/eval_jaxpr/ppermute | solution.py:19
  472.5 10.2 %collective-permute-start.2 = (bf16[4,128,128]{2,1,0:T(8,128)(2,1)S(1)}, bf16[4,128,128]{2,1,0:T(8,128)(2,1)S(1)}, u32[]{:S(2)}, u32[]{:S(2)}) collective-permute-start(bf16[4,128,128]{2,1,0:T(8,128)(2,1)S(1)} %get-tuple-element.674), channel_id=1, source_target_pairs={{1,0},{2,1},{3,2},{4,3},{5,4},{6,5},{7,6},{8,7},{9,8},{10,9},{11,1... | collective-permute-start | bytes 393224 | tf_op jit(solution)/shard_map/while/body/eval_jaxpr/ppermute | solution.py:22
  487.6 10.5 %collective-permute-start.4 = (bf16[16,128,128]{2,1,0:T(8,128)(2,1)S(1)}, bf16[16,128,128]{2,1,0:T(8,128)(2,1)S(1)}, u32[]{:S(2)}, u32[]{:S(2)}) collective-permute-start(bf16[16,128,128]{2,1,0:T(8,128)(2,1)S(1)} %get-tuple-element.676), channel_id=1, source_target_pairs={{0,32},{32,64},{64,96},{96,128},{128,160},{160,192},{192,224},{1,3... | collective-permute-start | bytes 1572872 | tf_op jit(solution)/shard_map/while/body/eval_jaxpr/ppermute | solution.py:30
  500.5 7.0 %collective-permute-start.1 = (bf16[4,128,128]{2,1,0:T(8,128)(2,1)S(1)}, bf16[4,128,128]{2,1,0:T(8,128)(2,1)}, u32[]{:S(2)}, u32[]{:S(2)}) collective-permute-start(bf16[4,128,128]{2,1,0:T(8,128)(2,1)S(1)} %get-tuple-element.672), channel_id=1, source_target_pairs={{0,1},{1,2},{2,3},{3,4},{4,5},{5,6},{6,7},{7,8},{8,9},{9,10},{10,1... | collective-permute-start | bytes 393224 | tf_op jit(solution)/shard_map/while/body/eval_jaxpr/ppermute | solution.py:19
  503.3 10.3 %collective-permute-start = (bf16[4,128,128]{2,1,0:T(8,128)(2,1)S(1)}, bf16[4,128,128]{2,1,0:T(8,128)(2,1)}, u32[]{:S(2)}, u32[]{:S(2)}) collective-permute-start(bf16[4,128,128]{2,1,0:T(8,128)(2,1)S(1)} %get-tuple-element.671), channel_id=1, source_target_pairs={{1,0},{2,1},{3,2},{4,3},{5,4},{6,5},{7,6},{8,7},{9,8},{10,9},{11,1... | collective-permute-start | bytes 393224 | tf_op jit(solution)/shard_map/while/body/eval_jaxpr/ppermute | solution.py:22
  520.1 7.0 %copy-start.8 = (bf16[16,128,128]{2,1,0:T(8,128)(2,1)S(1)}, bf16[16,128,128]{2,1,0:T(8,128)(2,1)}, u32[]{:S(2)}) copy-start(bf16[16,128,128]{2,1,0:T(8,128)(2,1)} %get-tuple-element.755) | copy-start | bytes 1572868 | tf_op jit(solution)/shard_map/while
  520.1 7.0 %collective-permute-start.3 = (bf16[4,128,128]{2,1,0:T(8,128)(2,1)S(1)}, bf16[4,128,128]{2,1,0:T(8,128)(2,1)S(1)}, u32[]{:S(2)}, u32[]{:S(2)}) collective-permute-start(bf16[4,128,128]{2,1,0:T(8,128)(2,1)S(1)} %get-tuple-element.675), channel_id=1, source_target_pairs={{0,1},{1,2},{2,3},{3,4},{4,5},{5,6},{6,7},{7,8},{8,9},{9,10},{10,1... | collective-permute-start | bytes 393224 | tf_op jit(solution)/shard_map/while/body/eval_jaxpr/ppermute | solution.py:19
  524.5 10.2 %collective-permute-start.2 = (bf16[4,128,128]{2,1,0:T(8,128)(2,1)S(1)}, bf16[4,128,128]{2,1,0:T(8,128)(2,1)S(1)}, u32[]{:S(2)}, u32[]{:S(2)}) collective-permute-start(bf16[4,128,128]{2,1,0:T(8,128)(2,1)S(1)} %get-tuple-element.674), channel_id=1, source_target_pairs={{1,0},{2,1},{3,2},{4,3},{5,4},{6,5},{7,6},{8,7},{9,8},{10,9},{11,1... | collective-permute-start | bytes 393224 | tf_op jit(solution)/shard_map/while/body/eval_jaxpr/ppermute | solution.py:22
  539.6 10.5 %collective-permute-start.4 = (bf16[16,128,128]{2,1,0:T(8,128)(2,1)S(1)}, bf16[16,128,128]{2,1,0:T(8,128)(2,1)S(1)}, u32[]{:S(2)}, u32[]{:S(2)}) collective-permute-start(bf16[16,128,128]{2,1,0:T(8,128)(2,1)S(1)} %get-tuple-element.676), channel_id=1, source_target_pairs={{0,32},{32,64},{64,96},{96,128},{128,160},{160,192},{192,224},{1,3... | collective-permute-start | bytes 1572872 | tf_op jit(solution)/shard_map/while/body/eval_jaxpr/ppermute | solution.py:30
  (159 other events, 334.5 us)
where the time goes:
time: 560 us; the launch traced here: 553 us
  waiting for transfers between devices  175 us (31%)
  starting transfers between devices  139 us (25%)
  matrix products  136 us (24%)
  local copies, waits for them, and re-layouts  76.1 us (14%)
  other arithmetic  23.7 us (4%)
    dot_general x180, matrix products, neuron_layer(): jnp.einsum('jrc,jce->jre', moved, dense, preferred_element_type=jnp.float32)  136 us
    ppermute x10, waiting for transfers between devices, passed_along(): lax.ppermute(value, axis, [(source, source + steps) for source in range(i...  85.7 us
    ppermute x20, waiting for transfers between devices, with_halo(): lax.ppermute(lax.slice_in_dim(block, 0, width, axis=dim), axis, backward)  75.7 us
    ppermute x20, starting transfers between devices, with_halo(): lax.ppermute(lax.slice_in_dim(block, block.shape[dim] - width, None, axis...  70.8 us
    ppermute x20, starting transfers between devices, with_halo(): lax.ppermute(lax.slice_in_dim(block, 0, width, axis=dim), axis, backward)  48.7 us
    while x340, local copies, waits for them, and re-layouts  44.4 us
    gather x10, local copies, waits for them, and re-layouts, advance(): jnp.take(sample_blocks, lax.dynamic_index_in_dim(order, entry_no, 0, keep...  21.1 us
    ppermute x10, starting transfers between devices, passed_along(): lax.ppermute(value, axis, [(source, source + steps) for source in range(i...  19.2 us
  transfers between devices with their start and end apart: 50, of which 50 were waited for; matrix products, arithmetic and copies ran while one was open for 10% of the time, Pallas kernels for 0%

commit v1 on v0

v1 whole, which is shorter than its diff:
```python
import functools

import jax
import jax.numpy as jnp
from jax import lax
from jax.experimental import pallas as pl
from jax.experimental.pallas import tpu as pltpu
from jax.sharding import PartitionSpec as P

MESH = pl.DeviceIdType.MESH
BLOCK = 128
KMAX = 5
REACH = 4
S = 128
NMB = 3
ROWS = 16
WIDE = 2 * REACH
EDGE = ROWS + 2 * REACH
XZERO = ROWS + 2 * WIDE
HZERO = EDGE
HSTEP = EDGE + 1
HALF = ROWS // 2
SAMPLES = S * NMB


def kernel(
    segments, neurons, piece,
    samples, batch, weights, bias_any, offset_any, count_any, bias, offset, count,
    out,
    wa, wb, raw, main, halo, mid, mid_out, result, x, h, bias_l, bias_r,
    off_l, off_r, cnt_l, cnt_r, ia, ib, pos,
    load_sem, info_send, info_recv, w_send, w_recv,
    main_send, main_recv, halo_send, halo_recv, fwd_send, mid_send, mid_recv, out_sem,
):
    pieces = SAMPLES // piece
    s = lax.axis_index("segment")
    n = lax.axis_index("neuron")
    left = lax.rem(n + neurons - 1, neurons)
    right = lax.rem(n + 1, neurons)
    odd = lax.rem(s, 2)
    first = s == 0
    even = odd == 0
    last = s == segments - 1
    pair = s + 1 - 2 * odd
    crossing = jnp.logical_not(first) & jnp.logical_not(last)
    other = jnp.clip(s - 1 + 2 * odd, 0, segments - 1)

    def remote(src, dst, send, recv, device):
        return pltpu.make_async_remote_copy(
            src_ref=src, dst_ref=dst, send_sem=send, recv_sem=recv,
            device_id=device, device_id_type=MESH,
        )

    load_a = pltpu.make_async_copy(weights.at[0], wa.at[pl.ds(REACH, ROWS)], load_sem.at[0])
    load_b = pltpu.make_async_copy(weights.at[1], wb, load_sem.at[1])
    load_s = pltpu.make_async_copy(samples, raw, load_sem.at[2])
    pl.when(first)(load_s.start)
    load_a.start()
    load_b.start()

    barrier = pltpu.get_barrier_semaphore()

    def greet(device):
        pl.semaphore_signal(barrier, inc=1, device_id=device, device_id_type=MESH)

    greet((s, left))
    greet((s, right))
    greet((pair, n))
    greet((pair, left))
    greet((pair, right))
    pl.when(crossing)(lambda: greet((other, n)))

    x[XZERO] = jnp.zeros((piece, BLOCK), jnp.bfloat16)
    for slot in range(2):
        h[slot * HSTEP + HZERO] = jnp.zeros((piece, BLOCK), jnp.bfloat16)

    @pl.when(first)
    def _():
        lanes = lax.broadcasted_iota(jnp.int32, (8, SAMPLES), 0)
        hot = jnp.where(jnp.broadcast_to(batch[...], (8, SAMPLES)) == lanes, 1.0, 0.0)
        before = jnp.where(
            lax.broadcasted_iota(jnp.int32, (SAMPLES, SAMPLES), 0)
            < lax.broadcasted_iota(jnp.int32, (SAMPLES, SAMPLES), 1),
            1.0, 0.0,
        ).astype(jnp.bfloat16)
        rank = jnp.dot(hot.astype(jnp.bfloat16), before, preferred_element_type=jnp.float32)
        place = hot * (rank + lanes.astype(jnp.float32) * float(S))
        pos[...] = jnp.broadcast_to(jnp.sum(place, axis=0, keepdims=True), (8, SAMPLES))

    pl.semaphore_wait(barrier, jnp.where(crossing, 6, 5))

    info = [
        remote(offset_any, off_r, info_send.at[0], info_recv.at[0], (s, left)),
        remote(offset_any, off_l, info_send.at[1], info_recv.at[1], (s, right)),
        remote(count_any, cnt_r, info_send.at[2], info_recv.at[2], (s, left)),
        remote(count_any, cnt_l, info_send.at[3], info_recv.at[3], (s, right)),
        remote(bias_any, bias_r, info_send.at[4], info_recv.at[4], (s, left)),
        remote(bias_any, bias_l, info_send.at[5], info_recv.at[5], (s, right)),
    ]
    rows_of_neighbours = [
        remote(
            weights.at[0, pl.ds(0, REACH)], wa.at[pl.ds(REACH + ROWS, REACH)],
            w_send.at[0], w_recv.at[0], (s, left),
        ),
        remote(
            weights.at[0, pl.ds(ROWS - REACH, REACH)], wa.at[pl.ds(0, REACH)],
            w_send.at[1], w_recv.at[1], (s, right),
        ),
    ]

    @pl.when(jnp.logical_not(first))
    def _():
        for copy in info:
            copy.start()
        for copy in rows_of_neighbours:
            copy.start()

    def main_copy(p, half, device):
        cols = pl.ds(half * HALF * BLOCK, HALF * BLOCK)
        return remote(
            result.at[p, :, cols], main.at[p, :, cols],
            main_send.at[p, half], main_recv.at[p, half], device,
        )

    def halo_copy(p, half, device):
        cols = pl.ds(half * HALF * BLOCK, HALF * BLOCK)
        return remote(
            result.at[p, :, cols], halo.at[p, 1 - half],
            halo_send.at[p, half], halo_recv.at[p, 1 - half], device,
        )

    def fwd_copy(p, half, device):
        cols = pl.ds(half * HALF * BLOCK, HALF * BLOCK)
        return remote(
            main.at[p, :, cols], halo.at[p, 1 - half],
            fwd_send.at[p, half], halo_recv.at[p, 1 - half], device,
        )

    def narrow_copy(p, half, device):
        width = REACH * BLOCK
        src = pl.ds(half * (ROWS - REACH) * BLOCK, width)
        dst = pl.ds((1 - half) * 0 + half * REACH * BLOCK, width)
        return remote(
            main.at[p, :, src], halo.at[p, 1 - half, :, dst],
            fwd_send.at[p, half], halo_recv.at[p, 1 - half], device,
        )

    def mid_copy(p, half, device):
        return remote(
            mid_out.at[p, half], mid.at[p, 1 - half],
            mid_send.at[p, half], mid_recv.at[p, 1 - half], device,
        )

    sides = ((0, (s, left)), (1, (s, right)))
    pair_sides = ((0, (pair, left)), (1, (pair, right)))

    def prepare(p):
        @pl.when(first)
        def _():
            want = lax.broadcasted_iota(jnp.int32, (piece, SAMPLES), 0) + p * piece
            pick = jnp.where(
                jnp.broadcast_to(pos[0:1, :], (piece, SAMPLES)) == want.astype(jnp.float32),
                1.0, 0.0,
            ).astype(jnp.bfloat16)
            for c in range(0, ROWS * BLOCK, 2 * BLOCK):
                main[p, :, c : c + 2 * BLOCK] = jnp.dot(
                    pick, raw[:, c : c + 2 * BLOCK], preferred_element_type=jnp.float32
                ).astype(jnp.bfloat16)
            for half, device in sides:
                narrow_copy(p, half, device).start()

        @pl.when(jnp.logical_not(first))
        def _():
            for half, device in sides:
                main_copy(p, half, (s, n)).wait_recv()
                fwd_copy(p, half, device).start()

    def first_rows(rows, slot, keep):
        for a in rows:
            taken = jnp.concatenate([x[ia[a * KMAX + k]] for k in range(KMAX)], axis=1)
            y = jnp.dot(
                taken, wa[a].reshape(KMAX * BLOCK, BLOCK), preferred_element_type=jnp.float32
            )
            j = a - REACH
            if j < 0:
                b = bias_l[0:1, (j + ROWS) * BLOCK : (j + ROWS + 1) * BLOCK]
            elif j < ROWS:
                b = bias[0:1, j * BLOCK : (j + 1) * BLOCK]
            else:
                b = bias_r[0:1, (j - ROWS) * BLOCK : (j - ROWS + 1) * BLOCK]
            y = jnp.maximum(y + b, 0.0).astype(jnp.bfloat16)
            h[slot * HSTEP + a] = y
            if keep is not None:
                keep(j, y)

    def second_rows(rows, slot, p):
        for j in rows:
            taken = jnp.concatenate(
                [h[slot * HSTEP + ib[j * KMAX + k]] for k in range(KMAX)], axis=1
            )
            y = jnp.dot(
                taken, wb[j].reshape(KMAX * BLOCK, BLOCK), preferred_element_type=jnp.float32
            )
            b = bias[1:2, j * BLOCK : (j + 1) * BLOCK]
            result[p, :, j * BLOCK : (j + 1) * BLOCK] = jnp.maximum(y + b, 0.0).astype(jnp.bfloat16)

    def stage_a(p):
        slot = lax.rem(p, 2)

        @pl.when(jnp.logical_not(even))
        def _():
            for half, _ in sides:
                main_copy(p, half, (pair, n)).wait_recv()

        for j in range(ROWS):
            x[WIDE + j] = main[p, :, j * BLOCK : (j + 1) * BLOCK]
        first_rows(range(2 * REACH, EDGE - 2 * REACH), slot, None)

        @pl.when(first)
        def _():
            for half, device in sides:
                narrow_copy(p, half, device).wait_recv()
            for j in range(REACH):
                c = (REACH + j) * BLOCK
                x[REACH + j] = halo[p, 0, :, c : c + BLOCK]
                x[WIDE + ROWS + j] = halo[p, 1, :, j * BLOCK : (j + 1) * BLOCK]

            def keep(j, y):
                half = 0 if j < REACH else 1
                c = (j - half * (ROWS - REACH)) * BLOCK
                mid_out[p, half, :, c : c + BLOCK] = y

            first_rows(range(REACH, 2 * REACH), slot, keep)
            first_rows(range(EDGE - 2 * REACH, EDGE - REACH), slot, keep)
            for half, device in sides:
                mid_copy(p, half, device).start()

        @pl.when(jnp.logical_not(first))
        def _():
            for half, device in sides:
                fwd_copy(p, half, device).wait_recv()
            for j in range(WIDE):
                x[j] = halo[p, 0, :, j * BLOCK : (j + 1) * BLOCK]
                x[WIDE + ROWS + j] = halo[p, 1, :, j * BLOCK : (j + 1) * BLOCK]
            first_rows(range(2 * REACH), slot, None)
            first_rows(range(EDGE - 2 * REACH, EDGE), slot, None)

    def stage_b(p):
        slot = lax.rem(p, 2)

        @pl.when(first)
        def _():
            for half, device in sides:
                mid_copy(p, half, device).wait_recv()
            for j in range(REACH):
                h[slot * HSTEP + j] = mid[p, 0, :, j * BLOCK : (j + 1) * BLOCK]
                h[slot * HSTEP + REACH + ROWS + j] = mid[p, 1, :, j * BLOCK : (j + 1) * BLOCK]

        for half in range(2):
            second_rows(range(half * HALF, (half + 1) * HALF), slot, p)

            @pl.when(even)
            def _():
                halo_copy(p, half, pair_sides[half][1]).start()
                main_copy(p, half, (pair, n)).start()

            @pl.when(jnp.logical_not(even) & jnp.logical_not(last))
            def _():
                main_copy(p, half, (other, n)).start()

        out_copy(p).start()

    def out_copy(p):
        return pltpu.make_async_copy(
            result.at[p], out.at[pl.ds(p * piece, piece), :], out_sem.at[p]
        )

    def fill(table, entry, off_ref, cnt_ref, layer, row, j, base, zero):
        used = cnt_ref[layer, row]
        for k in range(KMAX):
            off = off_ref[layer, row, k]
            place = n * ROWS + j + off
            live = (k < used) & (place >= 0) & (place < neurons * ROWS)
            table[entry * KMAX + k] = jnp.where(live, base + j + off, zero)

    def own(r, carry):
        fill(ia, r + REACH, offset, count, 0, r, r, WIDE, XZERO)
        fill(ib, r, offset, count, 1, r, r, REACH, HZERO)
        return carry

    lax.fori_loop(0, ROWS, own, 0)
    pl.when(first)(load_s.wait)
    pl.when(even)(lambda: prepare(0))

    @pl.when(jnp.logical_not(first))
    def _():
        for copy in info:
            copy.wait_recv()

        def sides_rows(r, carry):
            fill(ia, r, off_l, cnt_l, 0, ROWS - REACH + r, r - REACH, WIDE, XZERO)
            fill(ia, r + REACH + ROWS, off_r, cnt_r, 0, r, r + ROWS, WIDE, XZERO)
            return carry

        lax.fori_loop(0, REACH, sides_rows, 0)
        for copy in rows_of_neighbours:
            copy.wait_recv()

    load_a.wait()
    load_b.wait()

    def step(q, carry):
        @pl.when(q < pieces)
        def _():
            pl.when(even & (q + 1 < pieces))(lambda: prepare(q + 1))
            stage_a(q)

        p = q - jnp.where(first, 1, 0)
        pl.when((p >= 0) & (p < pieces))(lambda: stage_b(p))
        return carry

    lax.fori_loop(0, pieces + 1, step, 0)

    @pl.when(jnp.logical_not(first))
    def _():
        for copy in info:
            copy.wait_send()
        for copy in rows_of_neighbours:
            copy.wait_send()

    def drain(p, carry):
        out_copy(p).wait()
        for half in range(2):
            pl.when(jnp.logical_not(last))(lambda: main_copy(p, half, (pair, n)).wait_send())
            pl.when(even)(lambda: halo_copy(p, half, pair_sides[half][1]).wait_send())
            pl.when(first)(lambda: narrow_copy(p, half, sides[half][1]).wait_send())
            pl.when(first)(lambda: mid_copy(p, half, sides[half][1]).wait_send())
            pl.when(even & jnp.logical_not(first))(
                lambda: fwd_copy(p, half, sides[half][1]).wait_send()
            )
        return carry

    lax.fori_loop(0, pieces, drain, 0)


def solution(mesh):
    segments, neurons = mesh.shape["segment"], mesh.shape["neuron"]
    piece = 48
    pieces = SAMPLES // piece
    width = ROWS * BLOCK
    bf16, f32, i32 = jnp.bfloat16, jnp.float32, jnp.int32

    def on_device(samples, batch_of, weights, block_offset, block_count, bias):
        dma = pltpu.SemaphoreType.DMA
        vmem = pl.BlockSpec(memory_space=pltpu.VMEM)
        smem = pl.BlockSpec(memory_space=pltpu.SMEM)
        hbm = pl.BlockSpec(memory_space=pl.ANY)
        result = pl.pallas_call(
            functools.partial(kernel, segments, neurons, piece),
            out_shape=jax.ShapeDtypeStruct((SAMPLES, width), bf16),
            in_specs=[hbm, vmem, hbm, hbm, hbm, hbm, vmem, smem, smem],
            out_specs=hbm,
            scratch_shapes=[
                pltpu.VMEM((EDGE, KMAX, BLOCK, BLOCK), bf16),
                pltpu.VMEM((ROWS, KMAX, BLOCK, BLOCK), bf16),
                pltpu.VMEM((SAMPLES, width), bf16),
                pltpu.VMEM((pieces, piece, width), bf16),
                pltpu.VMEM((pieces, 2, piece, WIDE * BLOCK), bf16),
                pltpu.VMEM((pieces, 2, piece, REACH * BLOCK), bf16),
                pltpu.VMEM((pieces, 2, piece, REACH * BLOCK), bf16),
                pltpu.VMEM((pieces, piece, width), bf16),
                pltpu.VMEM((XZERO + 1, piece, BLOCK), bf16),
                pltpu.VMEM((2 * HSTEP, piece, BLOCK), bf16),
                pltpu.VMEM(bias.shape, f32),
                pltpu.VMEM(bias.shape, f32),
                pltpu.SMEM(block_offset.shape, i32),
                pltpu.SMEM(block_offset.shape, i32),
                pltpu.SMEM(block_count.shape, i32),
                pltpu.SMEM(block_count.shape, i32),
                pltpu.SMEM((EDGE * KMAX,), i32),
                pltpu.SMEM((ROWS * KMAX,), i32),
                pltpu.VMEM((8, SAMPLES), f32),
                dma((3,)), dma((6,)), dma((6,)), dma((2,)), dma((2,)),
                dma((pieces, 2)), dma((pieces, 2)), dma((pieces, 2)), dma((pieces, 2)),
                dma((pieces, 2)), dma((pieces, 2)), dma((pieces, 2)), dma((pieces,)),
            ],
            compiler_params=pltpu.CompilerParams(
                collective_id=0, has_side_effects=True, vmem_limit_bytes=56 << 20
            ),
        )(
            samples, batch_of.reshape(1, SAMPLES), weights, bias, block_offset, block_count,
            bias, block_offset, block_count,
        )
        return result.reshape(1, NMB, S, width)

    return jax.shard_map(
        on_device,
        mesh=mesh,
        in_specs=(
            P(None, "neuron"),
            P(),
            P("segment", "neuron", None, None, None),
            P("segment", "neuron", None),
            P("segment", "neuron"),
            P("segment", "neuron"),
        ),
        out_specs=P("segment", None, None, "neuron"),
        check_vma=False,
    )
```

time: 560 us -> 109 us (0.19)
  the two profiles are of different devices: /device:TPU:118 before, /device:TPU:25 now
where the time goes in v1:
time: 109 us; the launch traced here: 108 us
  Pallas kernels  103 us (94%)
  local copies, waits for them, and re-layouts  5.36 us (5%)
    pallas_call x1, Pallas kernels, on_device(): pl.pallas_call(functools.partial(kernel, segments, neurons, piece), out_s...  103 us
    unnamed x2, local copies, waits for them, and re-layouts  4.1 us

profile of v1, /device:TPU:25, one launch (start us, length us, event | category | flops | bytes accessed | tf_op | source)
XLA Modules:
  0.0 108.4 jit_solution(9061353436733548975)
XLA Ops:
  0.0 1.3 %reshape.6.batch = s32[1,384]{1,0:T(1,128)} reshape(s32[384]{0:T(512)} %param.7) | data formatting | bytes 3072 | tf_op jit(solution)/shard_map/reshape | solution.py:391
  1.3 1.4 %copy.7.offset_any.offset = s32[2,16,5]{2,1,0:T(8,128)} copy(s32[2,16,5]{1,0,2:T(2,128)} %param.9) | data formatting | bytes 1280 | tf_op args[3]
  2.6 103.0 %shard_map.64 = bf16[384,2048]{1,0:T(8,128)(2,1)} custom-call(bf16[384,2048]{1,0:T(8,128)(2,1)} %samples.1, s32[1,384]{1,0:T(1,128)} %reshape.6.batch, bf16[2,16,5,128,128]{4,3,2,1,0:T(8,128)(2,1)} %weights.1, f32[2,2048]{1,0:T(2,128)} %bias.1, s32[2,16,5]{2,1,0:T(8,128)} %copy.7.offset_any.offset, s32[2,16]{1,0:T(2,128)} %count.1, f32[2,2048]{1,0:T(2,128)} %bias.1, ...), custom_call_target="tpu_custom_call" | custom-call | tf_op jit(solution)/shard_map/pallas_call | solution.py:358
  105.6 2.7 %copy.10 = bf16[1,3,128,2048]{3,2,1,0:T(8,128)(2,1)} copy(bf16[1,3,128,2048]{3,2,1,0:T(8,128)(2,1)} %bitcast.1) | data formatting | bytes 3145728

commit v2 on v1

--- a/solution.py
+++ b/solution.py
@@ -21,6 +21,9 @@
 HSTEP = EDGE + 1
 HALF = ROWS // 2
 SAMPLES = S * NMB
+AHEAD = 2
+LAG = 2
+SLOTS = LAG + 1
 
 
 def kernel(
@@ -71,13 +74,13 @@
     pl.when(crossing)(lambda: greet((other, n)))
 
     x[XZERO] = jnp.zeros((piece, BLOCK), jnp.bfloat16)
-    for slot in range(2):
+    for slot in range(SLOTS):
         h[slot * HSTEP + HZERO] = jnp.zeros((piece, BLOCK), jnp.bfloat16)
 
     @pl.when(first)
     def _():
         lanes = lax.broadcasted_iota(jnp.int32, (8, SAMPLES), 0)
-        hot = jnp.where(jnp.broadcast_to(batch[...], (8, SAMPLES)) == lanes, 1.0, 0.0)
+        hot = jnp.where(jnp.broadcast_to(batch[...].reshape(1, SAMPLES), (8, SAMPLES)) == lanes, 1.0, 0.0)
         before = jnp.where(
             lax.broadcasted_iota(jnp.int32, (SAMPLES, SAMPLES), 0)
             < lax.broadcasted_iota(jnp.int32, (SAMPLES, SAMPLES), 1),
@@ -205,7 +208,7 @@
             result[p, :, j * BLOCK : (j + 1) * BLOCK] = jnp.maximum(y + b, 0.0).astype(jnp.bfloat16)
 
     def stage_a(p):
-        slot = lax.rem(p, 2)
+        slot = lax.rem(p, SLOTS)
 
         @pl.when(jnp.logical_not(even))
         def _():
@@ -246,7 +249,7 @@
             first_rows(range(EDGE - 2 * REACH, EDGE), slot, None)
 
     def stage_b(p):
-        slot = lax.rem(p, 2)
+        slot = lax.rem(p, SLOTS)
 
         @pl.when(first)
         def _():
@@ -278,7 +281,7 @@
     def fill(table, entry, off_ref, cnt_ref, layer, row, j, base, zero):
         used = cnt_ref[layer, row]
         for k in range(KMAX):
-            off = off_ref[layer, row, k]
+            off = off_ref[k, layer, row]
             place = n * ROWS + j + off
             live = (k < used) & (place >= 0) & (place < neurons * ROWS)
             table[entry * KMAX + k] = jnp.where(live, base + j + off, zero)
@@ -288,9 +291,13 @@
         fill(ib, r, offset, count, 1, r, r, REACH, HZERO)
         return carry
 
+    @pl.when(first)
+    def _():
+        load_s.wait()
+        for p in range(AHEAD):
+            prepare(p)
+
     lax.fori_loop(0, ROWS, own, 0)
-    pl.when(first)(load_s.wait)
-    pl.when(even)(lambda: prepare(0))
 
     @pl.when(jnp.logical_not(first))
     def _():
@@ -309,17 +316,22 @@
     load_a.wait()
     load_b.wait()
 
+    @pl.when(even & jnp.logical_not(first))
+    def _():
+        for p in range(AHEAD):
+            prepare(p)
+
     def step(q, carry):
         @pl.when(q < pieces)
         def _():
-            pl.when(even & (q + 1 < pieces))(lambda: prepare(q + 1))
+            pl.when(even & (q + AHEAD < pieces))(lambda: prepare(q + AHEAD))
             stage_a(q)
 
-        p = q - jnp.where(first, 1, 0)
+        p = q - jnp.where(first, LAG, 0)
         pl.when((p >= 0) & (p < pieces))(lambda: stage_b(p))
         return carry
 
-    lax.fori_loop(0, pieces + 1, step, 0)
+    lax.fori_loop(0, pieces + LAG, step, 0)
 
     @pl.when(jnp.logical_not(first))
     def _():
@@ -355,6 +367,7 @@
         vmem = pl.BlockSpec(memory_space=pltpu.VMEM)
         smem = pl.BlockSpec(memory_space=pltpu.SMEM)
         hbm = pl.BlockSpec(memory_space=pl.ANY)
+        offset = block_offset.transpose(2, 0, 1)
         result = pl.pallas_call(
             functools.partial(kernel, segments, neurons, piece),
             out_shape=jax.ShapeDtypeStruct((SAMPLES, width), bf16),
@@ -370,11 +383,11 @@
                 pltpu.VMEM((pieces, 2, piece, REACH * BLOCK), bf16),
                 pltpu.VMEM((pieces, piece, width), bf16),
                 pltpu.VMEM((XZERO + 1, piece, BLOCK), bf16),
-                pltpu.VMEM((2 * HSTEP, piece, BLOCK), bf16),
+                pltpu.VMEM((SLOTS * HSTEP, piece, BLOCK), bf16),
                 pltpu.VMEM(bias.shape, f32),
                 pltpu.VMEM(bias.shape, f32),
-                pltpu.SMEM(block_offset.shape, i32),
-                pltpu.SMEM(block_offset.shape, i32),
+                pltpu.SMEM(offset.shape, i32),
+                pltpu.SMEM(offset.shape, i32),
                 pltpu.SMEM(block_count.shape, i32),
                 pltpu.SMEM(block_count.shape, i32),
                 pltpu.SMEM((EDGE * KMAX,), i32),
@@ -388,8 +401,8 @@
                 collective_id=0, has_side_effects=True, vmem_limit_bytes=56 << 20
             ),
         )(
-            samples, batch_of.reshape(1, SAMPLES), weights, bias, block_offset, block_count,
-            bias, block_offset, block_count,
+            samples, batch_of, weights, bias, offset, block_count,
+            bias, offset, block_count,
         )
         return result.reshape(1, NMB, S, width)
 

time: 109 us -> 97.9 us (0.90)
  Pallas kernels: 103 us -> 95 us
  local copies, waits for them, and re-layouts: 5.36 us -> 2.73 us
    pallas_call x1, Pallas kernels: 103 us -> 95 us  [on_device(): pl.pallas_call(functools.partial(kernel, segments, neurons, piece), out_s...]
    unnamed x2 -> x1, local copies, waits for them, and re-layouts: 4.1 us -> 2.73 us
    reshape x1 -> x0, local copies, waits for them, and re-layouts: 1.25 us -> none  [on_device(): batch_of.reshape(1, SAMPLES)]
where the time goes in v2:
time: 97.9 us; the launch traced here: 97.8 us
  Pallas kernels  95 us (97%)
  local copies, waits for them, and re-layouts  2.73 us (3%)
    pallas_call x1, Pallas kernels, on_device(): pl.pallas_call(functools.partial(kernel, segments, neurons, piece), out_s...  95 us
    unnamed x1, local copies, waits for them, and re-layouts  2.73 us

profile of v2, /device:TPU:25, one launch (start us, length us, event | category | flops | bytes accessed | tf_op | source)
XLA Modules:
  0.0 97.8 jit_solution(12107568767266582967)
XLA Ops:
  0.0 95.0 %shard_map.64 = bf16[384,2048]{1,0:T(8,128)(2,1)} custom-call(bf16[384,2048]{1,0:T(8,128)(2,1)} %samples.1, s32[384]{0:T(512)} %batch.1, bf16[2,16,5,128,128]{4,3,2,1,0:T(8,128)(2,1)} %weights.1, f32[2,2048]{1,0:T(2,128)} %bias.1, s32[5,2,16]{2,1,0:T(2,128)} %bitcast.3, s32[2,16]{1,0:T(2,128)} %count.1, f32[2,2048]{1,0:T(2,128)} %bias.1, ...), custom_call_target="tpu_custom_call" | custom-call | tf_op jit(solution)/shard_map/pallas_call | solution.py:371
  95.0 2.7 %copy.8 = bf16[1,3,128,2048]{3,2,1,0:T(8,128)(2,1)} copy(bf16[1,3,128,2048]{3,2,1,0:T(8,128)(2,1)} %bitcast.2) | data formatting | bytes 3145728

commit v3 on v2

--- a/solution.py
+++ b/solution.py
@@ -38,8 +38,9 @@
     pieces = SAMPLES // piece
     s = lax.axis_index("segment")
     n = lax.axis_index("neuron")
-    left = lax.rem(n + neurons - 1, neurons)
-    right = lax.rem(n + 1, neurons)
+    left = jnp.maximum(n - 1, 0)
+    right = jnp.minimum(n + 1, neurons - 1)
+    there = (n > 0, n < neurons - 1)
     odd = lax.rem(s, 2)
     first = s == 0
     even = odd == 0
@@ -66,16 +67,34 @@
     def greet(device):
         pl.semaphore_signal(barrier, inc=1, device_id=device, device_id_type=MESH)
 
-    greet((s, left))
-    greet((s, right))
+    for side, neighbour in enumerate((left, right)):
+
+        @pl.when(there[side])
+        def _():
+            greet((s, neighbour))
+            greet((pair, neighbour))
+
     greet((pair, n))
-    greet((pair, left))
-    greet((pair, right))
     pl.when(crossing)(lambda: greet((other, n)))
 
-    x[XZERO] = jnp.zeros((piece, BLOCK), jnp.bfloat16)
+    blank = jnp.zeros((piece, BLOCK), jnp.bfloat16)
+    x[XZERO] = blank
     for slot in range(SLOTS):
-        h[slot * HSTEP + HZERO] = jnp.zeros((piece, BLOCK), jnp.bfloat16)
+        h[slot * HSTEP + HZERO] = blank
+    for side, (b_side, a_row) in enumerate(((bias_l, 0), (bias_r, REACH + ROWS))):
+
+        @pl.when(jnp.logical_not(there[side]))
+        def _():
+            for j in range(WIDE):
+                x[side * (WIDE + ROWS) + j] = blank
+            for slot in range(SLOTS):
+                for j in range(REACH):
+                    h[slot * HSTEP + a_row + j] = blank
+            b_side[...] = jnp.zeros(b_side.shape, jnp.float32)
+            for j in range(REACH):
+                wa[a_row + j] = jnp.zeros(wa.shape[1:], jnp.bfloat16)
+                for k in range(KMAX):
+                    ia[(a_row + j) * KMAX + k] = XZERO
 
     @pl.when(first)
     def _():
@@ -90,7 +109,10 @@
         place = hot * (rank + lanes.astype(jnp.float32) * float(S))
         pos[...] = jnp.broadcast_to(jnp.sum(place, axis=0, keepdims=True), (8, SAMPLES))
 
-    pl.semaphore_wait(barrier, jnp.where(crossing, 6, 5))
+    greeted = 1 + crossing.astype(jnp.int32)
+    for side in range(2):
+        greeted = greeted + 2 * there[side].astype(jnp.int32)
+    pl.semaphore_wait(barrier, greeted)
 
     info = [
         remote(offset_any, off_r, info_send.at[0], info_recv.at[0], (s, left)),
@@ -111,12 +133,13 @@
         ),
     ]
 
-    @pl.when(jnp.logical_not(first))
-    def _():
-        for copy in info:
-            copy.start()
-        for copy in rows_of_neighbours:
-            copy.start()
+    for side in range(2):
+
+        @pl.when(jnp.logical_not(first) & there[side])
+        def _():
+            for copy in info[side::2]:
+                copy.start()
+            rows_of_neighbours[side].start()
 
     def main_copy(p, half, device):
         cols = pl.ds(half * HALF * BLOCK, HALF * BLOCK)
@@ -142,7 +165,7 @@
     def narrow_copy(p, half, device):
         width = REACH * BLOCK
         src = pl.ds(half * (ROWS - REACH) * BLOCK, width)
-        dst = pl.ds((1 - half) * 0 + half * REACH * BLOCK, width)
+        dst = pl.ds(half * REACH * BLOCK, width)
         return remote(
             main.at[p, :, src], halo.at[p, 1 - half, :, dst],
             fwd_send.at[p, half], halo_recv.at[p, 1 - half], device,
@@ -170,13 +193,13 @@
                     pick, raw[:, c : c + 2 * BLOCK], preferred_element_type=jnp.float32
                 ).astype(jnp.bfloat16)
             for half, device in sides:
-                narrow_copy(p, half, device).start()
+                pl.when(there[half])(narrow_copy(p, half, device).start)
 
         @pl.when(jnp.logical_not(first))
         def _():
             for half, device in sides:
                 main_copy(p, half, (s, n)).wait_recv()
-                fwd_copy(p, half, device).start()
+                pl.when(there[half])(fwd_copy(p, half, device).start)
 
     def first_rows(rows, slot, keep):
         for a in rows:
@@ -221,12 +244,17 @@
 
         @pl.when(first)
         def _():
-            for half, device in sides:
-                narrow_copy(p, half, device).wait_recv()
-            for j in range(REACH):
-                c = (REACH + j) * BLOCK
-                x[REACH + j] = halo[p, 0, :, c : c + BLOCK]
-                x[WIDE + ROWS + j] = halo[p, 1, :, j * BLOCK : (j + 1) * BLOCK]
+            @pl.when(there[0])
+            def _():
+                narrow_copy(p, 1, (s, left)).wait_recv()
+                for j in range(REACH, WIDE):
+                    x[j] = halo[p, 0, :, j * BLOCK : (j + 1) * BLOCK]
+
+            @pl.when(there[1])
+            def _():
+                narrow_copy(p, 0, (s, right)).wait_recv()
+                for j in range(REACH):
+                    x[WIDE + ROWS + j] = halo[p, 1, :, j * BLOCK : (j + 1) * BLOCK]
 
             def keep(j, y):
                 half = 0 if j < REACH else 1
@@ -236,15 +264,17 @@
             first_rows(range(REACH, 2 * REACH), slot, keep)
             first_rows(range(EDGE - 2 * REACH, EDGE - REACH), slot, keep)
             for half, device in sides:
-                mid_copy(p, half, device).start()
+                pl.when(there[half])(mid_copy(p, half, device).start)
 
         @pl.when(jnp.logical_not(first))
         def _():
-            for half, device in sides:
-                fwd_copy(p, half, device).wait_recv()
-            for j in range(WIDE):
-                x[j] = halo[p, 0, :, j * BLOCK : (j + 1) * BLOCK]
-                x[WIDE + ROWS + j] = halo[p, 1, :, j * BLOCK : (j + 1) * BLOCK]
+            for side in range(2):
+
+                @pl.when(there[side])
+                def _():
+                    fwd_copy(p, 1 - side, sides[side][1]).wait_recv()
+                    for j in range(WIDE):
+                        x[side * (WIDE + ROWS) + j] = halo[p, side, :, j * BLOCK : (j + 1) * BLOCK]
             first_rows(range(2 * REACH), slot, None)
             first_rows(range(EDGE - 2 * REACH, EDGE), slot, None)
 
@@ -253,18 +283,22 @@
 
         @pl.when(first)
         def _():
-            for half, device in sides:
-                mid_copy(p, half, device).wait_recv()
-            for j in range(REACH):
-                h[slot * HSTEP + j] = mid[p, 0, :, j * BLOCK : (j + 1) * BLOCK]
-                h[slot * HSTEP + REACH + ROWS + j] = mid[p, 1, :, j * BLOCK : (j + 1) * BLOCK]
+            for side in range(2):
+
+                @pl.when(there[side])
+                def _():
+                    mid_copy(p, 1 - side, sides[side][1]).wait_recv()
+                    for j in range(REACH):
+                        h[slot * HSTEP + side * (REACH + ROWS) + j] = mid[
+                            p, side, :, j * BLOCK : (j + 1) * BLOCK
+                        ]
 
         for half in range(2):
             second_rows(range(half * HALF, (half + 1) * HALF), slot, p)
 
             @pl.when(even)
             def _():
-                halo_copy(p, half, pair_sides[half][1]).start()
+                pl.when(there[half])(halo_copy(p, half, pair_sides[half][1]).start)
                 main_copy(p, half, (pair, n)).start()
 
             @pl.when(jnp.logical_not(even) & jnp.logical_not(last))
@@ -301,17 +335,22 @@
 
     @pl.when(jnp.logical_not(first))
     def _():
-        for copy in info:
-            copy.wait_recv()
-
-        def sides_rows(r, carry):
-            fill(ia, r, off_l, cnt_l, 0, ROWS - REACH + r, r - REACH, WIDE, XZERO)
-            fill(ia, r + REACH + ROWS, off_r, cnt_r, 0, r, r + ROWS, WIDE, XZERO)
-            return carry
-
-        lax.fori_loop(0, REACH, sides_rows, 0)
-        for copy in rows_of_neighbours:
-            copy.wait_recv()
+        for side, (off_side, cnt_side, row) in enumerate(
+            ((off_l, cnt_l, ROWS - REACH), (off_r, cnt_r, 0))
+        ):
+
+            @pl.when(there[side])
+            def _():
+                for copy in info[1 - side :: 2]:
+                    copy.wait_recv()
+
+                def side_row(r, carry):
+                    j = r - REACH + side * (REACH + ROWS)
+                    fill(ia, j + REACH, off_side, cnt_side, 0, row + r, j, WIDE, XZERO)
+                    return carry
+
+                lax.fori_loop(0, REACH, side_row, 0)
+                rows_of_neighbours[1 - side].wait_recv()
 
     load_a.wait()
     load_b.wait()
@@ -333,23 +372,28 @@
 
     lax.fori_loop(0, pieces + LAG, step, 0)
 
-    @pl.when(jnp.logical_not(first))
-    def _():
-        for copy in info:
-            copy.wait_send()
-        for copy in rows_of_neighbours:
-            copy.wait_send()
+    for side in range(2):
+
+        @pl.when(jnp.logical_not(first) & there[side])
+        def _():
+            for copy in info[side::2]:
+                copy.wait_send()
+            rows_of_neighbours[side].wait_send()
 
     def drain(p, carry):
         out_copy(p).wait()
         for half in range(2):
             pl.when(jnp.logical_not(last))(lambda: main_copy(p, half, (pair, n)).wait_send())
-            pl.when(even)(lambda: halo_copy(p, half, pair_sides[half][1]).wait_send())
-            pl.when(first)(lambda: narrow_copy(p, half, sides[half][1]).wait_send())
-            pl.when(first)(lambda: mid_copy(p, half, sides[half][1]).wait_send())
-            pl.when(even & jnp.logical_not(first))(
-                lambda: fwd_copy(p, half, sides[half][1]).wait_send()
-            )
+
+            @pl.when(there[half])
+            def _():
+                pl.when(even)(lambda: halo_copy(p, half, pair_sides[half][1]).wait_send())
+                pl.when(first)(lambda: narrow_copy(p, half, sides[half][1]).wait_send())
+                pl.when(first)(lambda: mid_copy(p, half, sides[half][1]).wait_send())
+                pl.when(even & jnp.logical_not(first))(
+                    lambda: fwd_copy(p, half, sides[half][1]).wait_send()
+                )
+
         return carry
 
     lax.fori_loop(0, pieces, drain, 0)

time: 97.9 us -> 92.8 us (0.948)
  the two profiles are of different devices: /device:TPU:25 before, /device:TPU:127 now
where the time goes in v3:
time: 92.8 us; the launch traced here: 92.7 us
  Pallas kernels  89.9 us (97%)
  local copies, waits for them, and re-layouts  2.73 us (3%)
    pallas_call x1, Pallas kernels, on_device(): pl.pallas_call(functools.partial(kernel, segments, neurons, piece), out_s...  89.9 us
    unnamed x1, local copies, waits for them, and re-layouts  2.73 us

profile of v3, /device:TPU:127, one launch (start us, length us, event | category | flops | bytes accessed | tf_op | source)
XLA Modules:
  0.0 92.7 jit_solution(8295358853749058827)
XLA Ops:
  0.0 89.9 %shard_map.64 = bf16[384,2048]{1,0:T(8,128)(2,1)} custom-call(bf16[384,2048]{1,0:T(8,128)(2,1)} %samples.1, s32[384]{0:T(512)} %batch.1, bf16[2,16,5,128,128]{4,3,2,1,0:T(8,128)(2,1)} %weights.1, f32[2,2048]{1,0:T(2,128)} %bias.1, s32[5,2,16]{2,1,0:T(2,128)} %bitcast.3, s32[2,16]{1,0:T(2,128)} %count.1, f32[2,2048]{1,0:T(2,128)} %bias.1, ...), custom_call_target="tpu_custom_call" | custom-call | tf_op jit(solution)/shard_map/pallas_call | solution.py:415
  90.0 2.7 %copy.8 = bf16[1,3,128,2048]{3,2,1,0:T(8,128)(2,1)} copy(bf16[1,3,128,2048]{3,2,1,0:T(8,128)(2,1)} %bitcast.2) | data formatting | bytes 3145728

commit v4 on v3

--- a/solution.py
+++ b/solution.py
@@ -33,7 +33,7 @@
     wa, wb, raw, main, halo, mid, mid_out, result, x, h, bias_l, bias_r,
     off_l, off_r, cnt_l, cnt_r, ia, ib, pos,
     load_sem, info_send, info_recv, w_send, w_recv,
-    main_send, main_recv, halo_send, halo_recv, fwd_send, mid_send, mid_recv, out_sem,
+    main_send, main_recv, halo_send, halo_recv, fwd_send, mid_send, mid_recv, outer_send, outer_recv, out_sem,
 ):
     pieces = SAMPLES // piece
     s = lax.axis_index("segment")
@@ -148,11 +148,13 @@
             main_send.at[p, half], main_recv.at[p, half], device,
         )
 
-    def halo_copy(p, half, device):
-        cols = pl.ds(half * HALF * BLOCK, HALF * BLOCK)
+    def halo_copy(p, half, device, outer):
+        src = half * (ROWS - REACH) if outer else REACH + half * REACH
+        send, recv = (outer_send, outer_recv) if outer else (halo_send, halo_recv)
         return remote(
-            result.at[p, :, cols], halo.at[p, 1 - half],
-            halo_send.at[p, half], halo_recv.at[p, 1 - half], device,
+            result.at[p, :, pl.ds(src * BLOCK, REACH * BLOCK)],
+            halo.at[p, 1 - half, :, pl.ds((src - half * HALF) * BLOCK, REACH * BLOCK)],
+            send.at[p, half], recv.at[p, 1 - half], device,
         )
 
     def fwd_copy(p, half, device):
@@ -272,7 +274,13 @@
 
                 @pl.when(there[side])
                 def _():
-                    fwd_copy(p, 1 - side, sides[side][1]).wait_recv()
+                    pl.when(even)(fwd_copy(p, 1 - side, sides[side][1]).wait_recv)
+
+                    @pl.when(jnp.logical_not(even))
+                    def _():
+                        for outer in (True, False):
+                            halo_copy(p, 1 - side, pair_sides[side][1], outer).wait_recv()
+
                     for j in range(WIDE):
                         x[side * (WIDE + ROWS) + j] = halo[p, side, :, j * BLOCK : (j + 1) * BLOCK]
             first_rows(range(2 * REACH), slot, None)
@@ -293,17 +301,21 @@
                             p, side, :, j * BLOCK : (j + 1) * BLOCK
                         ]
 
-        for half in range(2):
-            second_rows(range(half * HALF, (half + 1) * HALF), slot, p)
-
-            @pl.when(even)
-            def _():
-                pl.when(there[half])(halo_copy(p, half, pair_sides[half][1]).start)
+        @pl.when(even)
+        def _():
+            ends = [*range(REACH), *range(ROWS - REACH, ROWS)]
+            for rows, outer in ((ends, True), (range(REACH, ROWS - REACH), False)):
+                second_rows(rows, slot, p)
+                for half, device in pair_sides:
+                    pl.when(there[half])(halo_copy(p, half, device, outer).start)
+            for half in range(2):
                 main_copy(p, half, (pair, n)).start()
 
-            @pl.when(jnp.logical_not(even) & jnp.logical_not(last))
-            def _():
-                main_copy(p, half, (other, n)).start()
+        @pl.when(jnp.logical_not(even))
+        def _():
+            for half in range(2):
+                second_rows(range(half * HALF, (half + 1) * HALF), slot, p)
+                pl.when(jnp.logical_not(last))(main_copy(p, half, (other, n)).start)
 
         out_copy(p).start()
 
@@ -387,7 +399,10 @@
 
             @pl.when(there[half])
             def _():
-                pl.when(even)(lambda: halo_copy(p, half, pair_sides[half][1]).wait_send())
+                for outer in (True, False):
+                    pl.when(even)(
+                        lambda: halo_copy(p, half, pair_sides[half][1], outer).wait_send()
+                    )
                 pl.when(first)(lambda: narrow_copy(p, half, sides[half][1]).wait_send())
                 pl.when(first)(lambda: mid_copy(p, half, sides[half][1]).wait_send())
                 pl.when(even & jnp.logical_not(first))(
@@ -439,7 +454,8 @@
                 pltpu.VMEM((8, SAMPLES), f32),
                 dma((3,)), dma((6,)), dma((6,)), dma((2,)), dma((2,)),
                 dma((pieces, 2)), dma((pieces, 2)), dma((pieces, 2)), dma((pieces, 2)),
-                dma((pieces, 2)), dma((pieces, 2)), dma((pieces, 2)), dma((pieces,)),
+                dma((pieces, 2)), dma((pieces, 2)), dma((pieces, 2)), dma((pieces, 2)), dma((pieces, 2)),
+                dma((pieces,)),
             ],
             compiler_params=pltpu.CompilerParams(
                 collective_id=0, has_side_effects=True, vmem_limit_bytes=56 << 20

time: 92.8 us -> 92.2 us (level)
  no operation moved by 1% of the time
where the time goes in v4:
time: 92.2 us; the launch traced here: 92 us
  Pallas kernels  89.3 us (97%)
  local copies, waits for them, and re-layouts  2.73 us (3%)
    pallas_call x1, Pallas kernels, on_device(): pl.pallas_call(functools.partial(kernel, segments, neurons, piece), out_s...  89.3 us
    unnamed x1, local copies, waits for them, and re-layouts  2.73 us

profile of v4, /device:TPU:127, one launch (start us, length us, event | category | flops | bytes accessed | tf_op | source)
XLA Modules:
  0.0 92.0 jit_solution(7312015728770171201)
XLA Ops:
  0.0 89.3 %shard_map.64 = bf16[384,2048]{1,0:T(8,128)(2,1)} custom-call(bf16[384,2048]{1,0:T(8,128)(2,1)} %samples.1, s32[384]{0:T(512)} %batch.1, bf16[2,16,5,128,128]{4,3,2,1,0:T(8,128)(2,1)} %weights.1, f32[2,2048]{1,0:T(2,128)} %bias.1, s32[5,2,16]{2,1,0:T(2,128)} %bitcast.3, s32[2,16]{1,0:T(2,128)} %count.1, f32[2,2048]{1,0:T(2,128)} %bias.1, ...), custom_call_target="tpu_custom_call" | custom-call | tf_op jit(solution)/shard_map/pallas_call | solution.py:430
  89.3 2.7 %copy.8 = bf16[1,3,128,2048]{3,2,1,0:T(8,128)(2,1)} copy(bf16[1,3,128,2048]{3,2,1,0:T(8,128)(2,1)} %bitcast.2) | data formatting | bytes 3145728

commit v5 on v4

--- a/solution.py
+++ b/solution.py
@@ -243,6 +243,8 @@
         for j in range(ROWS):
             x[WIDE + j] = main[p, :, j * BLOCK : (j + 1) * BLOCK]
         first_rows(range(2 * REACH, EDGE - 2 * REACH), slot, None)
+        relays = even & jnp.logical_not(first) & (p + AHEAD < pieces)
+        pl.when(relays)(lambda: prepare(p + AHEAD))
 
         @pl.when(first)
         def _():
@@ -375,7 +377,7 @@
     def step(q, carry):
         @pl.when(q < pieces)
         def _():
-            pl.when(even & (q + AHEAD < pieces))(lambda: prepare(q + AHEAD))
+            pl.when(first & (q + AHEAD < pieces))(lambda: prepare(q + AHEAD))
             stage_a(q)
 
         p = q - jnp.where(first, LAG, 0)

time: 92.2 us -> 91.8 us (level)
  no operation moved by 1% of the time
where the time goes in v5:
time: 91.8 us; the launch traced here: 91.6 us
  Pallas kernels  88.9 us (97%)
  local copies, waits for them, and re-layouts  2.73 us (3%)
    pallas_call x1, Pallas kernels, on_device(): pl.pallas_call(functools.partial(kernel, segments, neurons, piece), out_s...  88.9 us
    unnamed x1, local copies, waits for them, and re-layouts  2.73 us

profile of v5, /device:TPU:127, one launch (start us, length us, event | category | flops | bytes accessed | tf_op | source)
XLA Modules:
  0.0 91.6 jit_solution(2737916111381601113)
XLA Ops:
  0.0 88.9 %shard_map.64 = bf16[384,2048]{1,0:T(8,128)(2,1)} custom-call(bf16[384,2048]{1,0:T(8,128)(2,1)} %samples.1, s32[384]{0:T(512)} %batch.1, bf16[2,16,5,128,128]{4,3,2,1,0:T(8,128)(2,1)} %weights.1, f32[2,2048]{1,0:T(2,128)} %bias.1, s32[5,2,16]{2,1,0:T(2,128)} %bitcast.3, s32[2,16]{1,0:T(2,128)} %count.1, f32[2,2048]{1,0:T(2,128)} %bias.1, ...), custom_call_target="tpu_custom_call" | custom-call | tf_op jit(solution)/shard_map/pallas_call | solution.py:432
  88.9 2.7 %copy.8 = bf16[1,3,128,2048]{3,2,1,0:T(8,128)(2,1)} copy(bf16[1,3,128,2048]{3,2,1,0:T(8,128)(2,1)} %bitcast.2) | data formatting | bytes 3145728
